TPU v7x, 32 devices: a whole 2x2x4 slice. The times are simulated.
32 devices in a mesh: groups: 2 (over x), chan: 8 (over z, y), seq: 2 (over core).
Axes of the slice: x: 2, y: 2, z: 4, core: 2. Of those that a mesh axis runs over, the one named last changes fastest.
Arguments:
- tokens: bfloat16 [2048, 8192], P(('groups', 'seq'), 'chan'), parts along dimension 0, may hold values from -42 to 42
- norm_gain: float32 [8192], replicated, may hold values from 0.1 to 1.9
- in_weight: bfloat16 [3, 8192, 8192], P(None, None, 'chan'), may hold values from -0.0625 to 0.0625
- short_weight: float32 [3, 7, 8192], P(None, None, 'chan'), may hold values from -2 to 2
- log_decay: float32 [16, 8192], P(None, 'chan'), may hold values from -0.034 to 0
- residue: float32 [16, 8192], P(None, 'chan'), may hold values from -0.15625 to 0.15625
- skip: float32 [8192], P('chan'), may hold values from 0.1 to 1.9
- out_weight: bfloat16 [8192, 8192], P('chan'), may hold values from -0.09375 to 0.09375
Outputs:
- mixed: bfloat16 [2048, 8192], P(('groups', 'seq'), 'chan'), parts along dimension 0
There are 2 independent parts, one for each index of `groups`. A program takes and returns all parts, laid end to end along the dimension named above; an argument that names none is the same for every part. Nothing has to cross between parts.
All inputs are finite; a program needn't handle non-finite values.
Results may differ from a plain program's by a relative error of at most 0.0067.
Values may be sent and summed in bfloat16 or wider, within the bound.
No kernel may reach another device: no remote copies, remote signals or barrier semaphores. Data moves between devices by JAX's collectives and lax.ppermute only.
A program may use at most 448 MiB of HBM per device.

v0:
```python
import functools

import jax
import jax.numpy as jnp
from jax import lax
from jax.experimental import pallas as pl
from jax.experimental.pallas import tpu as pltpu
from jax.sharding import PartitionSpec as P

EPSILON = 1e-06
LANES = 128
KEEP = 8
VMEM_LIMIT = 48 * 1024 * 1024


def from_behind(block, axis, distance):
    count = lax.axis_size(axis)
    route = [(i - distance, i) for i in range(count) if i - distance >= 0]
    return lax.ppermute(block, axis, route)


def tree_sum(terms):
    while len(terms) > 1:
        pairs = [terms[i] + terms[i + 1] for i in range(0, len(terms) - 1, 2)]
        terms = pairs + terms[len(pairs) * 2 :]
    return terms[0]


def accumulate_kernel(depths, pairs, width, first, last, place_ref, *refs):
    chunk_refs, refs = refs[: len(depths) + sum(pairs)], refs[len(depths) + sum(pairs) :]
    gain_refs, refs = refs[: len(depths)], refs[len(depths) :]
    w_refs, refs = refs[: len(depths)], refs[len(depths) :]
    if not first:
        held_ref, held_sq_ref, refs = refs[0], refs[1], refs[2:]
    if last:
        acc_ref, sq_ref, rim_ref, scaled_ref = refs
    else:
        acc_ref, sq_ref, scaled_ref = refs
    feat, col = pl.program_id(0), pl.program_id(1)

    @pl.when((feat == 0) & (col == 0))
    def _():
        square = None if first else held_sq_ref[...]
        start = at = 0
        for j, depth in enumerate(depths):
            x = chunk_refs[at][...]
            at += 1
            if pairs[j]:
                x = jnp.where(place_ref[len(depths)] == 1, x, chunk_refs[at][...])
                at += 1
            x = x.astype(jnp.float32)
            parts = [x[:, g : g + LANES] * x[:, g : g + LANES] for g in range(0, depth, LANES)]
            part = tree_sum(parts)
            square = part if square is None else square + part
            scaled_ref[:, start : start + depth] = (x * gain_refs[j][0]).astype(jnp.bfloat16)
            start += depth
        if last:
            total = jnp.sum(square, axis=1, keepdims=True)
            square = jnp.broadcast_to(lax.rsqrt(total / width + EPSILON), square.shape)
        sq_ref[...] = square

    start, part = 0, None
    for j, depth in enumerate(depths):
        one = jnp.dot(scaled_ref[:, start : start + depth], w_refs[j][0], preferred_element_type=jnp.float32)
        part = one if part is None else part + one
        start += depth
    acc_ref[0] = part if first else held_ref[0] + part
    if last:
        keep = rim_ref.shape[1]
        rows = acc_ref.shape[1]
        rim = acc_ref[0, rows - keep :, :] * sq_ref[rows - keep :, :1]
        rim_ref[0] = rim.astype(jnp.bfloat16).astype(jnp.float32)


def accumulate(chunks, places, gain, in_weight, held=None, last=False, use_first=None):
    pairs = [isinstance(c, tuple) for c in chunks]
    arrays = [a for c in chunks for a in (c if isinstance(c, tuple) else (c,))]
    depths = [(c[0] if isinstance(c, tuple) else c).shape[1] for c in chunks]
    rows = arrays[0].shape[0]
    width, chans = in_weight.shape[1:]
    tile = min(512, chans)
    first = held is None
    acc_spec = pl.BlockSpec((1, rows, tile), lambda i, c, p: (i, 0, c))
    sq_spec = pl.BlockSpec((rows, LANES), lambda i, c, p: (0, 0))
    in_specs = [pl.BlockSpec(a.shape, lambda i, c, p: (0, 0)) for a in arrays]
    in_specs += [pl.BlockSpec((1, 1, d), lambda i, c, p, j=j: (p[j], 0, 0)) for j, d in enumerate(depths)]
    in_specs += [pl.BlockSpec((1, d, tile), lambda i, c, p, j=j: (i, p[j], c)) for j, d in enumerate(depths)]
    out_specs = [acc_spec, sq_spec]
    out_shape = [
        jax.ShapeDtypeStruct((3, rows, chans), jnp.float32),
        jax.ShapeDtypeStruct((rows, LANES), jnp.float32),
    ]
    if last:
        out_specs.append(pl.BlockSpec((1, KEEP, tile), lambda i, c, p: (i, 0, c)))
        out_shape.append(jax.ShapeDtypeStruct((3, KEEP, chans), jnp.float32))
    extra, aliases = (), {}
    if not first:
        in_specs += [acc_spec, sq_spec]
        extra = tuple(held)
        base = 1 + len(arrays) + 2 * len(depths)
        aliases = {base: 0, base + 1: 1}
    scalars = list(places) + ([] if use_first is None else [use_first])
    return pl.pallas_call(
        functools.partial(accumulate_kernel, depths, pairs, width, first, last),
        grid_spec=pltpu.PrefetchScalarGridSpec(
            num_scalar_prefetch=1,
            grid=(3, chans // tile),
            in_specs=in_specs,
            out_specs=out_specs,
            scratch_shapes=[pltpu.VMEM((rows, sum(depths)), jnp.bfloat16)],
        ),
        out_shape=out_shape,
        input_output_aliases=aliases,
        compiler_params=pltpu.CompilerParams(vmem_limit_bytes=26 * 1024 * 1024),
        cost_estimate=pl.CostEstimate(
            flops=rows * sum(depths) * chans,
            bytes_accessed=6 * sum(depths) * chans,
            transcendentals=0,
        ),
        name="accumulate",
    )(
        jnp.stack([jnp.asarray(n, jnp.int32) for n in scalars]),
        *arrays,
        *[gain.reshape(-1, 1, d) for d in depths],
        *[in_weight] * len(depths),
        *extra,
    )


def pieces_kernel(count, place_ref, gated_ref, w_ref, *refs):
    outs = refs[-count:]
    total = jnp.dot(gated_ref[...], w_ref[...], preferred_element_type=jnp.float32)
    for j in range(count):

        @pl.when(pl.program_id(0) == j)
        def _():
            outs[j][...] = total.astype(outs[j].dtype)


def pieces(out_weight, gated, wanted, *earlier):
    rows, chans = gated.shape
    count = len(wanted)
    out = pl.pallas_call(
        functools.partial(pieces_kernel, count),
        grid_spec=pltpu.PrefetchScalarGridSpec(
            num_scalar_prefetch=1,
            grid=(count,),
            in_specs=[
                pl.BlockSpec((rows, chans), lambda t, p: (0, 0)),
                pl.BlockSpec((chans, chans), lambda t, p: (0, p[t])),
            ]
            + [pl.BlockSpec(memory_space=pl.ANY)] * len(earlier),
            out_specs=[pl.BlockSpec((rows, chans), lambda t, p: (0, 0))] * count,
        ),
        out_shape=[jax.ShapeDtypeStruct((rows, chans), dtype) for place, dtype in wanted],
        compiler_params=pltpu.CompilerParams(vmem_limit_bytes=VMEM_LIMIT),
        cost_estimate=pl.CostEstimate(flops=count * 1000000, bytes_accessed=count * 100000, transcendentals=0),
        name="pieces",
    )(jnp.stack([place.astype(jnp.int32) for place, dtype in wanted]), gated, out_weight, *earlier)
    return list(out)


def finish_kernel(*refs):
    out_ref = refs[-1]
    count = (len(refs) - 1) // 2
    step, per_half = pl.program_id(0), pl.num_programs(0) // 2

    for h in range(2):

        @pl.when((step >= h * per_half) & (step < (h + 1) * per_half))
        def _():
            total = refs[h * count][...].astype(jnp.float32)
            for ref in refs[h * count + 1 : (h + 1) * count]:
                total = total + ref[...].astype(jnp.float32)
            out_ref[...] = total.astype(jnp.bfloat16)


def finish(upper, lower):
    rows, chans = upper[0].shape
    blk = min(128, rows)
    per_half = rows // blk
    spec = lambda h: pl.BlockSpec((blk, chans), lambda t: (jnp.clip(t - h * per_half, 0, per_half - 1), 0))
    return pl.pallas_call(
        finish_kernel,
        grid=(2 * per_half,),
        in_specs=[spec(0)] * len(upper) + [spec(1)] * len(lower),
        out_specs=pl.BlockSpec((blk, chans), lambda t: (t, 0)),
        out_shape=jax.ShapeDtypeStruct((2 * rows, chans), jnp.bfloat16),
        compiler_params=pltpu.CompilerParams(vmem_limit_bytes=VMEM_LIMIT),
        name="finish",
    )(*upper, *lower)


def along_line(block, pairs):
    return lax.ppermute(block, "chan", [(2 * a + y, 2 * b + y) for a, b in pairs for y in (0, 1)])


def after(block, *earlier):
    return lax.optimization_barrier((block,) + earlier)[0]


def across(block, *earlier):
    count = lax.axis_size("chan")
    if earlier:
        block = after(block, *earlier)
    return lax.ppermute(block, "chan", [(c, c ^ 1) for c in range(count)])


def total(*terms):
    return functools.reduce(lambda a, b: a + b, [t.astype(jnp.float32) for t in terms])


PAIRS = [(0, 1), (1, 0), (2, 3), (3, 2)]
MIDDLE = [(1, 2), (2, 1)]
OUTWARD = [(1, 0), (2, 3)]
INWARD = [(0, 1), (3, 2)]


def gather_and_project(tokens, gain, in_weight, params):
    me = lax.axis_index("chan")
    half = tokens.shape[1] // 2
    at_end = (me < 2) | (me >= 6)
    own_over = across(tokens)
    next_one = along_line(tokens, PAIRS)
    middle = along_line(tokens, MIDDLE)
    held = accumulate([tokens], [me], gain, in_weight)
    next_over = across(next_one, own_over, held[1])
    second_out = along_line(after(middle, held[1]), OUTWARD)
    second_mid = along_line(after(next_one, held[1]), MIDDLE)
    held = accumulate([own_over, next_one], [me ^ 1, me ^ 2], gain, in_weight, held)
    second = jnp.where(at_end, second_out, second_mid)
    second_over = across(second, next_over, held[1])
    third_out = along_line(after(second_mid, second_out, held[1]), OUTWARD)
    rest_mid = along_line(after(own_over[:, half:], second_mid, held[1]), MIDDLE)
    held = accumulate([next_over, second], [me ^ 3, me ^ 4], gain, in_weight, held)
    third = jnp.where(at_end, third_out, middle)
    third_over = across(third[:, :half], second_over, held[1])
    rest_out = along_line(after(second_over[:, half:], held[1]), OUTWARD)
    square, *params = lax.optimization_barrier((held[1], *params))
    held = (held[0], square)
    held = accumulate([second_over, third], [me ^ 5, me ^ 6], gain, in_weight, held)
    last = [third_over, (rest_out, rest_mid)]
    place = (me ^ 7) * 2
    return accumulate(last, [place, place + 1], gain, in_weight, held, last=True, use_first=at_end), params


def project_and_reduce(gated, out_weight, tokens):
    me = lax.axis_index("chan")
    half = tokens.shape[0] // 2
    send = lambda k: (me ^ (2 * k + 1), jnp.bfloat16)
    keep = lambda k: (me ^ (2 * k), jnp.float32)
    narrow = lambda a: a.astype(jnp.bfloat16)
    make = functools.partial(pieces, out_weight)
    both = (0, 1)

    upper = gated(0)
    third_send_0 = make(upper, [send(3)])[0]
    third_over = across(third_send_0)
    lower = gated(1, third_send_0)
    third_send_1 = make(lower, [send(3)])[0]
    rest_in = along_line(third_send_1, INWARD)
    rest_mid = along_line(third_send_1, MIDDLE)
    second_send_0, third_keep_0 = make(upper, [send(2), keep(3)], third_send_1)
    second_send_1, third_1 = make(lower, [send(2), (keep(3)[0], jnp.bfloat16)], second_send_0)
    third = [narrow(total(third_keep_0, third_over)), third_1]
    third_in = [along_line(third[h], INWARD) for h in both]
    second_send = [second_send_0, narrow(total(second_send_1, rest_in))]
    second_over = [across(second_send[h], third_over) for h in both]
    halves = (upper, lower)
    later = [make(halves[h], [keep(2), send(1)], third_1) for h in both]
    second = [narrow(total(later[h][0], second_over[h], third_in[h])) for h in both]
    second_in = [along_line(second[h], INWARD) for h in both]
    second_mid = [along_line(second[h], MIDDLE) for h in both]
    next_over = [across(later[h][1], second_over[h]) for h in both]
    later = [make(halves[h], [keep(1), send(0)], third_over) for h in both]
    own_send = [later[0][1], narrow(total(later[1][1], rest_mid))]
    next_one = [narrow(total(later[h][0], next_over[h], second_mid[h])) for h in both]
    next_in = [along_line(next_one[h], PAIRS) for h in both]
    middle_in = [along_line(narrow(total(third[h], second_in[h])), MIDDLE) for h in both]
    own_over = [across(own_send[h], next_over[h]) for h in both]
    own_keep = [make(halves[h], [keep(0)], second_over[0])[0] for h in both]
    base = [total(own_keep[h], tokens[h * half : (h + 1) * half]) for h in both]
    return finish(*[[base[h], own_over[h], next_in[h], middle_in[h]] for h in both])


def mix_kernel(
    acc_ref, rms_ref, rim_ref, taps_ref, decay_ref, res_ref, skip_ref, q_ref, base_ref, end_ref, win_ref, prod_ref, state_ref
):
    step = pl.program_id(0)
    rows = acc_ref.shape[1]
    groups = taps_ref.shape[2]
    tap_count = taps_ref.shape[1]
    poles = decay_ref.shape[0]
    keep = rim_ref.shape[1]
    unroll = 8

    @pl.when(step == 0)
    def _():
        for g in range(groups):
            win_ref[:, :keep, g, :] = rim_ref[:, :, g * LANES : (g + 1) * LANES]
        state_ref[...] = jnp.zeros_like(state_ref)

    inv_rms = rms_ref[:, :1]
    for i in range(3):
        for g in range(groups):
            cols = acc_ref[i, :, g * LANES : (g + 1) * LANES] * inv_rms
            win_ref[i, keep:, g, :] = cols.astype(jnp.bfloat16).astype(jnp.float32)

    def convolve(blk, nothing):
        first = blk * unroll
        conv = []
        for i in range(3):
            taps = [taps_ref[i, j] for j in range(tap_count)]
            held = [win_ref[i, first + keep - (tap_count - 1) + r] for r in range(unroll + tap_count - 1)]
            conv.append(
                [
                    functools.reduce(
                        lambda a, b: a + b, [taps[j] * held[r + tap_count - 1 - j] for j in range(tap_count)]
                    )
                    for r in range(unroll)
                ]
            )
        for r in range(unroll):
            q_ref[first + r] = conv[0][r]
            prod_ref[first + r] = conv[1][r] * conv[2][r]
        return nothing

    lax.fori_loop(0, rows // unroll, convolve, 0)
    win_ref[:, :keep] = win_ref[:, rows:]
    decay = [jnp.exp(decay_ref[n]) for n in range(poles)]
    res = [res_ref[n] for n in range(poles)]
    skip = skip_ref[0]

    def recur(blk, state):
        state = list(state)
        for r in range(unroll):
            t = blk * unroll + r
            product = prod_ref[t]
            sums = [skip * product]
            for n in range(poles):
                state[n] = decay[n] * state[n] + product
                term = res[n] * state[n]
                if n < 3:
                    sums.append(term)
                else:
                    sums[n % 4] = sums[n % 4] + term
            base_ref[t] = q_ref[t] * tree_sum(sums)
        return tuple(state)

    state = lax.fori_loop(0, rows // unroll, recur, tuple(state_ref[n] for n in range(poles)))
    for n in range(poles):
        state_ref[n] = state[n]

    @pl.when(step == pl.num_programs(0) - 1)
    def _():
        for n in range(poles):
            end_ref[n] = state[n]


def mix(acc, inv_rms, rim, taps, log_decay, residue, skip):
    rows, chans = acc.shape[1:]
    groups = chans // LANES
    tap_count, poles = taps.shape[1], log_decay.shape[0]
    keep = rim.shape[1]
    blk = min(128, rows)
    whole = lambda *shape: pl.BlockSpec(shape, lambda t: (0,) * len(shape))
    row_spec = pl.BlockSpec((blk, groups, LANES), lambda t: (t, 0, 0))
    return pl.pallas_call(
        mix_kernel,
        grid=(rows // blk,),
        in_specs=[
            pl.BlockSpec((3, blk, chans), lambda t: (0, t, 0)),
            pl.BlockSpec((blk, LANES), lambda t: (t, 0)),
            whole(3, keep, chans),
            whole(3, tap_count, groups, LANES),
            whole(poles, groups, LANES),
            whole(poles, groups, LANES),
            whole(1, groups, LANES),
        ],
        out_specs=[row_spec, row_spec, whole(poles, groups, LANES)],
        out_shape=[
            jax.ShapeDtypeStruct((rows, groups, LANES), jnp.float32),
            jax.ShapeDtypeStruct((rows, groups, LANES), jnp.float32),
            jax.ShapeDtypeStruct((poles, groups, LANES), jnp.float32),
        ],
        scratch_shapes=[
            pltpu.VMEM((3, keep + blk, groups, LANES), jnp.float32),
            pltpu.VMEM((blk, groups, LANES), jnp.float32),
            pltpu.VMEM((poles, groups, LANES), jnp.float32),
        ],
        compiler_params=pltpu.CompilerParams(vmem_limit_bytes=26 * 1024 * 1024),
        cost_estimate=pl.CostEstimate(
            flops=110 * rows * groups * LANES, bytes_accessed=20 * rows * groups * LANES, transcendentals=0
        ),
        name="mix",
    )(acc, inv_rms, rim, taps, log_decay, residue, skip)


def carry_kernel(start, q_ref, base_ref, state_ref, decay_ref, res_ref, *refs):
    out_ref, coef_ref, row_ref = refs[-3:]
    step = pl.program_id(0)
    rows, groups = q_ref.shape[:2]
    poles = decay_ref.shape[0]
    decay = [jnp.exp(decay_ref[n]) for n in range(poles)]

    @pl.when(step == 0)
    def _():
        for n in range(poles):
            coef_ref[n] = res_ref[n] * (jnp.exp((start + 1.0) * decay_ref[n]) * state_ref[n])

    unroll = 8

    def body(blk, coef):
        coef = list(coef)
        for r in range(unroll):
            t = blk * unroll + r
            row_ref[t] = base_ref[t] + q_ref[t] * tree_sum(list(coef))
            for n in range(poles):
                coef[n] = decay[n] * coef[n]
        return tuple(coef)

    coef = lax.fori_loop(0, rows // unroll, body, tuple(coef_ref[n] for n in range(poles)))
    for n in range(poles):
        coef_ref[n] = coef[n]
    for g in range(groups):
        out_ref[:, g * LANES : (g + 1) * LANES] = row_ref[:, g, :].astype(jnp.bfloat16)


def carry(query, base, state, log_decay, residue, start, rows, *earlier):
    groups = query.shape[1]
    poles = log_decay.shape[0]
    blk = min(128, rows)
    whole = lambda *shape: pl.BlockSpec(shape, lambda t: (0,) * len(shape))
    row_spec = pl.BlockSpec((blk, groups, LANES), lambda t: (t + start // blk, 0, 0))
    return pl.pallas_call(
        functools.partial(carry_kernel, start),
        grid=(rows // blk,),
        in_specs=[row_spec, row_spec]
        + [whole(poles, groups, LANES)] * 3
        + [pl.BlockSpec(memory_space=pl.ANY)] * len(earlier),
        out_specs=pl.BlockSpec((blk, groups * LANES), lambda t: (t, 0)),
        out_shape=jax.ShapeDtypeStruct((rows, groups * LANES), jnp.bfloat16),
        scratch_shapes=[
            pltpu.VMEM((poles, groups, LANES), jnp.float32),
            pltpu.VMEM((blk, groups, LANES), jnp.float32),
        ],
        compiler_params=pltpu.CompilerParams(vmem_limit_bytes=26 * 1024 * 1024),
        cost_estimate=pl.CostEstimate(
            flops=40 * rows * groups * LANES, bytes_accessed=80 * rows * groups * LANES, transcendentals=0
        ),
        name="carry",
    )(query, base, state, log_decay, residue, *earlier)


def per_device(tokens, norm_gain, in_weight, short_weight, log_decay, residue, skip, out_weight):
    rows, chans = tokens.shape
    groups = chans // LANES
    by_lane = lambda a: a.reshape(a.shape[:-1] + (groups, LANES))
    taps, log_decay, residue = by_lane(short_weight), by_lane(log_decay), by_lane(residue)
    skip = by_lane(skip[None, :])

    paired_line = lax.axis_size("chan") == 8
    if paired_line:
        params = (taps, log_decay, residue, skip)
        (acc, inv_rms, rim), params = gather_and_project(tokens, norm_gain, in_weight, params)
        taps, log_decay, residue, skip = params
    else:
        gathered = lax.all_gather(tokens, "chan", axis=1, tiled=True)
        depth = min(1024, gathered.shape[1])
        parts = [gathered[:, k : k + depth] for k in range(0, gathered.shape[1], depth)]
        held = None
        for k, part in enumerate(parts):
            held = accumulate([part], [k], norm_gain, in_weight, held, last=k == len(parts) - 1)
        acc, inv_rms, rim = held
    rim = from_behind(rim, "seq", 1)
    query, base, end = mix(acc, inv_rms, rim, taps, log_decay, residue, skip)
    shard_decay = jnp.exp(rows * log_decay)
    state, passing = jnp.zeros_like(end), end
    for _ in range(lax.axis_size("seq") - 1):
        passing = from_behind(passing, "seq", 1)
        state = state + passing
        passing = passing * shard_decay
    if paired_line:

        def half_gated(h, *earlier):
            return carry(query, base, state, log_decay, residue, h * rows // 2, rows // 2, *earlier)

        return project_and_reduce(half_gated, out_weight, tokens)
    gated = carry(query, base, state, log_decay, residue, 0, rows)
    partial = jnp.dot(gated, out_weight, preferred_element_type=jnp.float32)
    branch = lax.psum_scatter(partial.astype(jnp.bfloat16), "chan", scatter_dimension=1, tiled=True)
    return (tokens.astype(jnp.float32) + branch.astype(jnp.float32)).astype(jnp.bfloat16)


def solution(mesh):
    return jax.shard_map(
        per_device,
        mesh=mesh,
        in_specs=(
            P(("groups", "seq"), "chan"),
            P(),
            P(None, None, "chan"),
            P(None, None, "chan"),
            P(None, "chan"),
            P(None, "chan"),
            P("chan"),
            P("chan", None),
        ),
        out_specs=P(("groups", "seq"), "chan"),
        check_vma=False,
    )
```

profile of v0, /device:TPU:0, one launch (start us, length us, event | category | flops | bytes accessed | tf_op | source)
XLA Modules:
  0.0 237.6 jit_solution(3441590346245971698)
XLA Ops:
  0.7 5.8 %collective-permute-start = (bf16[512,1024]{1,0:T(8,128)(2,1)}, bf16[512,1024]{1,0:T(8,128)(2,1)S(1)}, u32[]{:S(2)}, u32[]{:S(2)}) collective-permute-start(bf16[512,1024]{1,0:T(8,128)(2,1)} %refs_0_.1), channel_id=1, source_target_pairs={{0,4},{2,6},{4,0},{6,2},{8,12},{10,14},{12,8},{14,10},{1,5},{3,7},... | collective-permute-start | bytes 3145736 | tf_op jit(solution)/shard_map/ppermute | solution.py:195
  10.1 7.3 %accumulate.5 = (f32[3,512,1024]{2,1,0:T(8,128)S(1)}, f32[512,128]{1,0:T(8,128)S(1)}) custom-call(s32[1]{0:T(128)} %bitcast.place_ref, bf16[512,1024]{1,0:T(8,128)(2,1)S(1)} %copy-done.8, f32[8,1,1024]{2,1,0:T(1,128)S(1)} %bitcast.18, bf16[3,8192,1024]{2,1,0:T(8,128)(2,1)} %refs_6_.1), custom_call_target="tpu_custom_call" | custom-call | flops 536870912 | bytes 6291456 | tf_op jit(solution)/shard_map/accumulate/pallas_call | solution.py:103
  17.4 2.7 %copy-done = f32[3,512,1024]{2,1,0:T(8,128)} copy-done((f32[3,512,1024]{2,1,0:T(8,128)}, f32[3,512,1024]{2,1,0:T(8,128)S(1)}, u32[]{:S(2)}) %copy-start) | copy-done | bytes 6291480
  20.1 9.6 %collective-permute-done.refs_1_ = bf16[512,1024]{1,0:T(8,128)(2,1)S(1)} collective-permute-done((bf16[512,1024]{1,0:T(8,128)(2,1)}, bf16[512,1024]{1,0:T(8,128)(2,1)S(1)}, u32[]{:S(2)}, u32[]{:S(2)}) %collective-permute-start) | collective-permute-done | bytes 1048608 | tf_op jit(solution)/shard_map/ppermute | solution.py:195
  34.3 2.8 %copy-done.1 = f32[3,512,1024]{2,1,0:T(8,128)S(1)} copy-done((f32[3,512,1024]{2,1,0:T(8,128)S(1)}, f32[3,512,1024]{2,1,0:T(8,128)}, u32[]{:S(2)}) %copy-start.1) | copy-done | bytes 6291480
  37.0 11.4 %accumulate.6 = (f32[3,512,1024]{2,1,0:T(8,128)S(1)}, f32[512,128]{1,0:T(8,128)S(1)}) custom-call(s32[2]{0:T(128)S(1)} %pad_add_fusion.1.place_ref, bf16[512,1024]{1,0:T(8,128)(2,1)S(1)} %collective-permute-done.4.refs_0_, bf16[512,1024]{1,0:T(8,128)(2,1)S(1)} %collective-permute-done.refs_1_, ...), custom_call_target="tpu_custom_call", output_to_operand_aliasing={{0}: (7, {}), {1}: (8, {})} | custom-call | flops 1073741824 | bytes 12582912 | tf_op jit(solution)/shard_map/accumulate/pallas_call | solution.py:103
  48.5 2.7 %copy-done.2 = f32[3,512,1024]{2,1,0:T(8,128)} copy-done((f32[3,512,1024]{2,1,0:T(8,128)}, f32[3,512,1024]{2,1,0:T(8,128)S(1)}, u32[]{:S(2)}) %copy-start.2) | copy-done | bytes 6291480
  51.2 6.1 %collective-permute-done.3 = bf16[512,1024]{1,0:T(8,128)(2,1)} collective-permute-done((bf16[512,1024]{1,0:T(8,128)(2,1)S(1)}, bf16[512,1024]{1,0:T(8,128)(2,1)}, u32[]{:S(2)}, u32[]{:S(2)}) %collective-permute-start.3) | collective-permute-done | bytes 1048608 | tf_op jit(solution)/shard_map/ppermute | solution.py:195
  63.9 2.8 %copy-done.3 = f32[3,512,1024]{2,1,0:T(8,128)S(1)} copy-done((f32[3,512,1024]{2,1,0:T(8,128)S(1)}, f32[3,512,1024]{2,1,0:T(8,128)}, u32[]{:S(2)}) %copy-start.3) | copy-done | bytes 6291480
  66.7 11.8 %accumulate.7 = (f32[3,512,1024]{2,1,0:T(8,128)S(1)}, f32[512,128]{1,0:T(8,128)S(1)}) custom-call(s32[2]{0:T(128)S(1)} %pad_add_fusion.2.place_ref, bf16[512,1024]{1,0:T(8,128)(2,1)} %collective-permute-done.6.refs_0_, bf16[512,1024]{1,0:T(8,128)(2,1)S(1)} %broadcast_select_fusion.refs_1_, ...), custom_call_target="tpu_custom_call", output_to_operand_aliasing={{0}: (7, {}), {1}: (8, {})} | custom-call | flops 1073741824 | bytes 12582912 | tf_op jit(solution)/shard_map/accumulate/pallas_call | solution.py:103
  78.5 2.7 %copy-done.4 = f32[3,512,1024]{2,1,0:T(8,128)} copy-done((f32[3,512,1024]{2,1,0:T(8,128)}, f32[3,512,1024]{2,1,0:T(8,128)S(1)}, u32[]{:S(2)}) %copy-start.4) | copy-done | bytes 6291480
  90.5 2.8 %copy-done.5 = f32[3,512,1024]{2,1,0:T(8,128)S(1)} copy-done((f32[3,512,1024]{2,1,0:T(8,128)S(1)}, f32[3,512,1024]{2,1,0:T(8,128)}, u32[]{:S(2)}) %copy-start.5) | copy-done | bytes 6291480
  93.2 11.4 %accumulate.8 = (f32[3,512,1024]{2,1,0:T(8,128)S(1)}, f32[512,128]{1,0:T(8,128)S(1)}) custom-call(s32[2]{0:T(128)S(1)} %pad_add_fusion.3.place_ref, bf16[512,1024]{1,0:T(8,128)(2,1)S(1)} %collective-permute-done.7.refs_0_, bf16[512,1024]{1,0:T(8,128)(2,1)S(1)} %broadcast_select_fusion.1.refs_1_, ...), custom_call_target="tpu_custom_call", output_to_operand_aliasing={{0}: (7, {}), {1}: (8, {})} | custom-call | flops 1073741824 | bytes 12582912 | tf_op jit(solution)/shard_map/accumulate/pallas_call | solution.py:103
  104.7 8.4 %accumulate.9 = (f32[3,512,1024]{2,1,0:T(8,128)S(1)}, f32[512,128]{1,0:T(8,128)S(1)}, f32[3,8,1024]{2,1,0:T(8,128)S(1)}) custom-call(s32[3]{0:T(128)S(1)} %pad_add_fusion.place_ref, bf16[512,512]{1,0:T(8,128)(2,1)} %collective-permute-done.8.refs_0_, ...), custom_call_target="tpu_custom_call", output_to_operand_aliasing={{0}: (8, {}), {1}: (9, {})} | custom-call | flops 536870912 | bytes 6291456 | tf_op jit(solution)/shard_map/accumulate/pallas_call | solution.py:103
  113.1 2.7 %copy-done.6 = f32[3,512,1024]{2,1,0:T(8,128)} copy-done((f32[3,512,1024]{2,1,0:T(8,128)}, f32[3,512,1024]{2,1,0:T(8,128)S(1)}, u32[]{:S(2)}) %copy-start.6) | copy-done | bytes 6291480
  118.0 2.8 %copy-done.7 = f32[3,512,1024]{2,1,0:T(8,128)S(1)} copy-done((f32[3,512,1024]{2,1,0:T(8,128)S(1)}, f32[3,512,1024]{2,1,0:T(8,128)}, u32[]{:S(2)}) %copy-start.7) | copy-done | bytes 6291480
  120.8 13.1 %mix.1 = (f32[512,8,128]{2,1,0:T(8,128)S(1)}, f32[512,8,128]{2,1,0:T(8,128)S(1)}, f32[16,8,128]{2,1,0:T(8,128)S(1)}) custom-call(f32[3,512,1024]{2,1,0:T(8,128)S(1)} %copy-done.7, f32[512,128]{1,0:T(8,128)S(1)} %get-tuple-element.68.rms_ref, f32[3,8,1024]{2,1,0:T(8,128)S(1)} %collective-permute-done.11.rim_ref, f32[3,7,8,128]{3,2,1,0:T(8,128)S(1)} %reshape.24.taps_ref, ...), custom_call_target="tpu_custom_call" | custom-call | flops 57671680 | bytes 10485760 | tf_op jit(solution)/shard_map/mix/pallas_call | solution.py:368
  133.9 2.4 %collective-permute-start.12 = (f32[16,8,128]{2,1,0:T(8,128)S(1)}, f32[16,8,128]{2,1,0:T(8,128)S(1)}, u32[]{:S(2)}, u32[]{:S(2)}) collective-permute-start(f32[16,8,128]{2,1,0:T(8,128)S(1)} %get-tuple-element.76), channel_id=1, source_target_pairs={{0,1},{2,3},{4,5},{6,7},{8,9},{10,11},{12,13},{14,15},{16,17},{18,... | collective-permute-start | bytes 196616 | tf_op jit(solution)/shard_map/ppermute | solution.py:19
  147.0 4.6 %collective-permute-start.23 = (bf16[256,1024]{1,0:T(8,128)(2,1)S(1)}, bf16[256,1024]{1,0:T(8,128)(2,1)S(1)}, u32[]{:S(2)}, u32[]{:S(2)}) collective-permute-start(bf16[256,1024]{1,0:T(8,128)(2,1)S(1)} %pieces.11.refs_0_), channel_id=1, source_target_pairs={{0,4},{2,6},{12,8},{14,10},{1,5},{3,7},{13,9},{15,11},{16,20},{18,... | collective-permute-start | bytes 1572872 | tf_op jit(solution)/shard_map/ppermute | solution.py:195
  151.6 3.7 %pieces.12 = (bf16[256,1024]{1,0:T(8,128)(2,1)S(1)}, f32[256,1024]{1,0:T(8,128)S(1)}) custom-call(s32[2]{0:T(128)S(1)} %pad_add_fusion.3.place_ref, bf16[256,1024]{1,0:T(8,128)(2,1)S(1)} %carry.2.gated_ref, bf16[1024,8192]{1,0:T(8,128)(2,1)} %w_ref.19, bf16[256,1024]{1,0:T(8,128)(2,1)S(1)} %pieces.11.refs_0_), custom_call_target="tpu_custom_call" | custom-call | flops 2000000 | bytes 200000 | tf_op jit(solution)/shard_map/pieces/pallas_call | solution.py:143
  157.1 4.2 %collective-permute-start.17 = (bf16[256,1024]{1,0:T(8,128)(2,1)S(1)}, bf16[256,1024]{1,0:T(8,128)(2,1)S(1)}, u32[]{:S(2)}, u32[]{:S(2)}) collective-permute-start(bf16[256,1024]{1,0:T(8,128)(2,1)S(1)} %add_convert_fusion.8), channel_id=1, source_target_pairs={{0,4},{2,6},{12,8},{14,10},{1,5},{3,7},{13,9},{15,11},{16,20},{18,... | collective-permute-start | bytes 1572872 | tf_op jit(solution)/shard_map/ppermute | solution.py:195
  162.1 3.7 %pieces.15 = (bf16[256,1024]{1,0:T(8,128)(2,1)S(1)}, bf16[256,1024]{1,0:T(8,128)(2,1)S(1)}) custom-call(s32[2]{0:T(128)S(1)} %pad_add_fusion.3.place_ref, bf16[256,1024]{1,0:T(8,128)(2,1)S(1)} %carry.3.gated_ref, bf16[1024,8192]{1,0:T(8,128)(2,1)} %w_ref.19, bf16[256,1024]{1,0:T(8,128)(2,1)S(1)} %get-tuple-element.78.refs_0_), custom_call_target="tpu_custom_call" | custom-call | flops 2000000 | bytes 200000 | tf_op jit(solution)/shard_map/pieces/pallas_call | solution.py:143
  165.8 3.3 %collective-permute-start.27 = (bf16[256,1024]{1,0:T(8,128)(2,1)S(1)}, bf16[256,1024]{1,0:T(8,128)(2,1)S(1)}, u32[]{:S(2)}, u32[]{:S(2)}) collective-permute-start(bf16[256,1024]{1,0:T(8,128)(2,1)S(1)} %get-tuple-element.80.refs_0_), channel_id=1, source_target_pairs={{0,4},{2,6},{12,8},{14,10},{1,5},{3,7},{13,9},{15,11},{16,20},{18,... | collective-permute-start | bytes 1572872 | tf_op jit(solution)/shard_map/ppermute | solution.py:195
  169.1 3.7 %pieces.16 = (f32[256,1024]{1,0:T(8,128)S(1)}, bf16[256,1024]{1,0:T(8,128)(2,1)S(1)}) custom-call(s32[2]{0:T(128)S(1)} %pad_add_fusion.5.place_ref, bf16[256,1024]{1,0:T(8,128)(2,1)S(1)} %carry.2.gated_ref, bf16[1024,8192]{1,0:T(8,128)(2,1)} %w_ref.19, bf16[256,1024]{1,0:T(8,128)(2,1)S(1)} %get-tuple-element.80.refs_0_), custom_call_target="tpu_custom_call" | custom-call | flops 2000000 | bytes 200000 | tf_op jit(solution)/shard_map/pieces/pallas_call | solution.py:143
  172.8 3.7 %pieces.19 = (f32[256,1024]{1,0:T(8,128)S(1)}, bf16[256,1024]{1,0:T(8,128)(2,1)S(1)}) custom-call(s32[2]{0:T(128)S(1)} %pad_add_fusion.5.place_ref, bf16[256,1024]{1,0:T(8,128)(2,1)S(1)} %carry.3.gated_ref, bf16[1024,8192]{1,0:T(8,128)(2,1)} %w_ref.19, bf16[256,1024]{1,0:T(8,128)(2,1)S(1)} %get-tuple-element.80.refs_0_), custom_call_target="tpu_custom_call" | custom-call | flops 2000000 | bytes 200000 | tf_op jit(solution)/shard_map/pieces/pallas_call | solution.py:143
  178.3 3.7 %pieces.18 = (f32[256,1024]{1,0:T(8,128)S(1)}, bf16[256,1024]{1,0:T(8,128)(2,1)S(1)}) custom-call(s32[2]{0:T(128)S(1)} %pad_add_fusion.4.place_ref, bf16[256,1024]{1,0:T(8,128)(2,1)S(1)} %carry.3.gated_ref, bf16[1024,8192]{1,0:T(8,128)(2,1)} %w_ref.19, bf16[256,1024]{1,0:T(8,128)(2,1)S(1)} %collective-permute-done.13.refs_0_), custom_call_target="tpu_custom_call" | custom-call | flops 2000000 | bytes 200000 | tf_op jit(solution)/shard_map/pieces/pallas_call | solution.py:143
  181.9 3.7 %pieces.14 = (f32[256,1024]{1,0:T(8,128)S(1)}, bf16[256,1024]{1,0:T(8,128)(2,1)S(1)}) custom-call(s32[2]{0:T(128)S(1)} %pad_add_fusion.4.place_ref, bf16[256,1024]{1,0:T(8,128)(2,1)S(1)} %carry.2.gated_ref, bf16[1024,8192]{1,0:T(8,128)(2,1)} %w_ref.19, bf16[256,1024]{1,0:T(8,128)(2,1)S(1)} %collective-permute-done.13.refs_0_), custom_call_target="tpu_custom_call" | custom-call | flops 2000000 | bytes 200000 | tf_op jit(solution)/shard_map/pieces/pallas_call | solution.py:143
  188.7 2.9 %collective-permute-done.24 = bf16[256,1024]{1,0:T(8,128)(2,1)S(1)} collective-permute-done((bf16[256,1024]{1,0:T(8,128)(2,1)S(1)}, bf16[256,1024]{1,0:T(8,128)(2,1)S(1)}, u32[]{:S(2)}, u32[]{:S(2)}) %collective-permute-start.24) | collective-permute-done | bytes 524320 | tf_op jit(solution)/shard_map/ppermute | solution.py:206
  193.9 6.6 %collective-permute-done.15 = bf16[256,1024]{1,0:T(8,128)(2,1)S(1)} collective-permute-done((bf16[256,1024]{1,0:T(8,128)(2,1)S(1)}, bf16[256,1024]{1,0:T(8,128)(2,1)S(1)}, u32[]{:S(2)}, u32[]{:S(2)}) %collective-permute-start.15) | collective-permute-done | bytes 524320 | tf_op jit(solution)/shard_map/ppermute | solution.py:206
  203.7 11.6 %collective-permute-done.25 = bf16[256,1024]{1,0:T(8,128)(2,1)S(1)} collective-permute-done((bf16[256,1024]{1,0:T(8,128)(2,1)S(1)}, bf16[256,1024]{1,0:T(8,128)(2,1)S(1)}, u32[]{:S(2)}, u32[]{:S(2)}) %collective-permute-start.25) | collective-permute-done | bytes 524320 | tf_op jit(solution)/shard_map/ppermute | solution.py:206
  218.1 8.5 %collective-permute-done.16.refs_1_ = bf16[256,1024]{1,0:T(8,128)(2,1)S(1)} collective-permute-done((bf16[256,1024]{1,0:T(8,128)(2,1)S(1)}, bf16[256,1024]{1,0:T(8,128)(2,1)S(1)}, u32[]{:S(2)}, u32[]{:S(2)}) %collective-permute-start.16) | collective-permute-done | bytes 524320 | tf_op jit(solution)/shard_map/ppermute | solution.py:206
  231.7 2.9 %collective-permute-done.26.refs_5_ = bf16[256,1024]{1,0:T(8,128)(2,1)S(1)} collective-permute-done((bf16[256,1024]{1,0:T(8,128)(2,1)S(1)}, bf16[256,1024]{1,0:T(8,128)(2,1)S(1)}, u32[]{:S(2)}, u32[]{:S(2)}) %collective-permute-start.26) | collective-permute-done | bytes 524320 | tf_op jit(solution)/shard_map/ppermute | solution.py:206
  (107 shorter events, 61.0 us)
Async XLA Ops:
  0.0 20.1 %collective-permute-start.2 = (bf16[512,1024]{1,0:T(8,128)(2,1)}, bf16[512,1024]{1,0:T(8,128)(2,1)S(1)}, u32[]{:S(2)}, u32[]{:S(2)}) collective-permute-start(bf16[512,1024]{1,0:T(8,128)(2,1)} %refs_0_.1), channel_id=1, source_target_pairs={{4,8},{6,10},{8,4},{10,6},{5,9},{7,11},{9,5},{11,7},{20,24},{22,26... | collective-permute-start | bytes 3145736 | tf_op jit(solution)/shard_map/ppermute | solution.py:195
  0.7 28.9 %collective-permute-start = (bf16[512,1024]{1,0:T(8,128)(2,1)}, bf16[512,1024]{1,0:T(8,128)(2,1)S(1)}, u32[]{:S(2)}, u32[]{:S(2)}) collective-permute-start(bf16[512,1024]{1,0:T(8,128)(2,1)} %refs_0_.1), channel_id=1, source_target_pairs={{0,4},{2,6},{4,0},{6,2},{8,12},{10,14},{12,8},{14,10},{1,5},{3,7},... | collective-permute-start | bytes 3145736 | tf_op jit(solution)/shard_map/ppermute | solution.py:195
  6.6 26.0 %collective-permute-start.4 = (bf16[512,1024]{1,0:T(8,128)(2,1)}, bf16[512,1024]{1,0:T(8,128)(2,1)S(1)}, u32[]{:S(2)}, u32[]{:S(2)}) collective-permute-start(bf16[512,1024]{1,0:T(8,128)(2,1)} %refs_0_.1), channel_id=1, source_target_pairs={{0,2},{2,0},{4,6},{6,4},{8,10},{10,8},{12,14},{14,12},{1,3},{3,1},... | collective-permute-start | bytes 3145736 | tf_op jit(solution)/shard_map/ppermute | solution.py:206
  29.7 21.5 %collective-permute-start.1 = (bf16[512,1024]{1,0:T(8,128)(2,1)S(1)}, bf16[512,1024]{1,0:T(8,128)(2,1)}, u32[]{:S(2)}, u32[]{:S(2)}) collective-permute-start(bf16[512,1024]{1,0:T(8,128)(2,1)S(1)} %collective-permute-done.refs_1_), channel_id=1, source_target_pairs={{4,8},{6,10},{8,4},{10,6},{5,9},{7,11},{9,5},{11,7},{20,24},{22,26... | collective-permute-start | bytes 3145736 | tf_op jit(solution)/shard_map/ppermute | solution.py:195
  31.3 26.0 %collective-permute-start.3 = (bf16[512,1024]{1,0:T(8,128)(2,1)S(1)}, bf16[512,1024]{1,0:T(8,128)(2,1)}, u32[]{:S(2)}, u32[]{:S(2)}) collective-permute-start(bf16[512,1024]{1,0:T(8,128)(2,1)S(1)} %collective-permute-done.2), channel_id=1, source_target_pairs={{4,0},{6,2},{8,12},{10,14},{5,1},{7,3},{9,13},{11,15},{20,16},{22,... | collective-permute-start | bytes 3145736 | tf_op jit(solution)/shard_map/ppermute | solution.py:195
  32.6 27.4 %collective-permute-start.6 = (bf16[512,1024]{1,0:T(8,128)(2,1)S(1)}, bf16[512,1024]{1,0:T(8,128)(2,1)}, u32[]{:S(2)}, u32[]{:S(2)}) collective-permute-start(bf16[512,1024]{1,0:T(8,128)(2,1)S(1)} %collective-permute-done.refs_1_), channel_id=1, source_target_pairs={{0,2},{2,0},{4,6},{6,4},{8,10},{10,8},{12,14},{14,12},{1,3},{3,1},... | collective-permute-start | bytes 3145736 | tf_op jit(solution)/shard_map/ppermute | solution.py:206
  57.3 25.3 %collective-permute-start.5 = (bf16[512,1024]{1,0:T(8,128)(2,1)}, bf16[512,1024]{1,0:T(8,128)(2,1)}, u32[]{:S(2)}, u32[]{:S(2)}) collective-permute-start(bf16[512,1024]{1,0:T(8,128)(2,1)} %collective-permute-done.1), channel_id=1, source_target_pairs={{4,0},{6,2},{8,12},{10,14},{5,1},{7,3},{9,13},{11,15},{20,16},{22,... | collective-permute-start | bytes 3145736 | tf_op jit(solution)/shard_map/ppermute | solution.py:195
  60.0 24.9 %collective-permute-start.7 = (bf16[512,1024]{1,0:T(8,128)(2,1)S(1)}, bf16[512,1024]{1,0:T(8,128)(2,1)S(1)}, u32[]{:S(2)}, u32[]{:S(2)}) collective-permute-start(bf16[512,1024]{1,0:T(8,128)(2,1)S(1)} %broadcast_select_fusion.refs_1_), channel_id=1, source_target_pairs={{0,2},{2,0},{4,6},{6,4},{8,10},{10,8},{12,14},{14,12},{1,3},{3,1},... | collective-permute-start | bytes 3145736 | tf_op jit(solution)/shard_map/ppermute | solution.py:206
  62.5 42.2 %collective-permute-start.10 = (bf16[512,512]{1,0:T(8,128)(2,1)}, bf16[512,512]{1,0:T(8,128)(2,1)}, u32[]{:S(2)}, u32[]{:S(2)}) collective-permute-start(bf16[512,512]{1,0:T(8,128)(2,1)} %slice.22), channel_id=1, source_target_pairs={{4,8},{6,10},{8,4},{10,6},{5,9},{7,11},{9,5},{11,7},{20,24},{22,26... | collective-permute-start | bytes 1572872 | tf_op jit(solution)/shard_map/ppermute | solution.py:195
  85.7 19.0 %collective-permute-start.9 = (bf16[512,512]{1,0:T(8,128)(2,1)}, bf16[512,512]{1,0:T(8,128)(2,1)S(1)}, u32[]{:S(2)}, u32[]{:S(2)}) collective-permute-start(bf16[512,512]{1,0:T(8,128)(2,1)} %slice.21), channel_id=1, source_target_pairs={{4,0},{6,2},{8,12},{10,14},{5,1},{7,3},{9,13},{11,15},{20,16},{22,... | collective-permute-start | bytes 1572872 | tf_op jit(solution)/shard_map/ppermute | solution.py:195
  87.0 17.7 %collective-permute-start.8 = (bf16[512,512]{1,0:T(8,128)(2,1)}, bf16[512,512]{1,0:T(8,128)(2,1)}, u32[]{:S(2)}, u32[]{:S(2)}) collective-permute-start(bf16[512,512]{1,0:T(8,128)(2,1)} %slice.20), channel_id=1, source_target_pairs={{0,2},{2,0},{4,6},{6,4},{8,10},{10,8},{12,14},{14,12},{1,3},{3,1},... | collective-permute-start | bytes 1572872 | tf_op jit(solution)/shard_map/ppermute | solution.py:206
  115.8 2.2 collective-permute-start.11
  133.9 3.2 %collective-permute-start.12 = (f32[16,8,128]{2,1,0:T(8,128)S(1)}, f32[16,8,128]{2,1,0:T(8,128)S(1)}, u32[]{:S(2)}, u32[]{:S(2)}) collective-permute-start(f32[16,8,128]{2,1,0:T(8,128)S(1)} %get-tuple-element.76), channel_id=1, source_target_pairs={{0,1},{2,3},{4,5},{6,7},{8,9},{10,11},{12,13},{14,15},{16,17},{18,... | collective-permute-start | bytes 196616 | tf_op jit(solution)/shard_map/ppermute | solution.py:19
  141.8 14.2 %collective-permute-start.13 = (bf16[256,1024]{1,0:T(8,128)(2,1)S(1)}, bf16[256,1024]{1,0:T(8,128)(2,1)S(1)}, u32[]{:S(2)}, u32[]{:S(2)}) collective-permute-start(bf16[256,1024]{1,0:T(8,128)(2,1)S(1)} %pieces.10.refs_0_), channel_id=1, source_target_pairs={{0,2},{2,0},{4,6},{6,4},{8,10},{10,8},{12,14},{14,12},{1,3},{3,1},... | collective-permute-start | bytes 1572872 | tf_op jit(solution)/shard_map/ppermute | solution.py:206
  147.0 29.5 %collective-permute-start.23 = (bf16[256,1024]{1,0:T(8,128)(2,1)S(1)}, bf16[256,1024]{1,0:T(8,128)(2,1)S(1)}, u32[]{:S(2)}, u32[]{:S(2)}) collective-permute-start(bf16[256,1024]{1,0:T(8,128)(2,1)S(1)} %pieces.11.refs_0_), channel_id=1, source_target_pairs={{0,4},{2,6},{12,8},{14,10},{1,5},{3,7},{13,9},{15,11},{16,20},{18,... | collective-permute-start | bytes 1572872 | tf_op jit(solution)/shard_map/ppermute | solution.py:195
  156.0 29.6 %collective-permute-start.14 = (bf16[256,1024]{1,0:T(8,128)(2,1)S(1)}, bf16[256,1024]{1,0:T(8,128)(2,1)S(1)}, u32[]{:S(2)}, u32[]{:S(2)}) collective-permute-start(bf16[256,1024]{1,0:T(8,128)(2,1)S(1)} %get-tuple-element.78.refs_0_), channel_id=1, source_target_pairs={{0,2},{2,0},{4,6},{6,4},{8,10},{10,8},{12,14},{14,12},{1,3},{3,1},... | collective-permute-start | bytes 1572872 | tf_op jit(solution)/shard_map/ppermute | solution.py:206
  157.1 29.2 %collective-permute-start.17 = (bf16[256,1024]{1,0:T(8,128)(2,1)S(1)}, bf16[256,1024]{1,0:T(8,128)(2,1)S(1)}, u32[]{:S(2)}, u32[]{:S(2)}) collective-permute-start(bf16[256,1024]{1,0:T(8,128)(2,1)S(1)} %add_convert_fusion.8), channel_id=1, source_target_pairs={{0,4},{2,6},{12,8},{14,10},{1,5},{3,7},{13,9},{15,11},{16,20},{18,... | collective-permute-start | bytes 1572872 | tf_op jit(solution)/shard_map/ppermute | solution.py:195
  161.4 26.4 %collective-permute-start.22 = (bf16[256,1024]{1,0:T(8,128)(2,1)S(1)}, bf16[256,1024]{1,0:T(8,128)(2,1)S(1)}, u32[]{:S(2)}, u32[]{:S(2)}) collective-permute-start(bf16[256,1024]{1,0:T(8,128)(2,1)S(1)} %pieces.11.refs_0_), channel_id=1, source_target_pairs={{4,8},{6,10},{8,4},{10,6},{5,9},{7,11},{9,5},{11,7},{20,24},{22,26... | collective-permute-start | bytes 1572872 | tf_op jit(solution)/shard_map/ppermute | solution.py:195
  165.8 22.9 %collective-permute-start.27 = (bf16[256,1024]{1,0:T(8,128)(2,1)S(1)}, bf16[256,1024]{1,0:T(8,128)(2,1)S(1)}, u32[]{:S(2)}, u32[]{:S(2)}) collective-permute-start(bf16[256,1024]{1,0:T(8,128)(2,1)S(1)} %get-tuple-element.80.refs_0_), channel_id=1, source_target_pairs={{0,4},{2,6},{12,8},{14,10},{1,5},{3,7},{13,9},{15,11},{16,20},{18,... | collective-permute-start | bytes 1572872 | tf_op jit(solution)/shard_map/ppermute | solution.py:195
  176.7 14.9 %collective-permute-start.24 = (bf16[256,1024]{1,0:T(8,128)(2,1)S(1)}, bf16[256,1024]{1,0:T(8,128)(2,1)S(1)}, u32[]{:S(2)}, u32[]{:S(2)}) collective-permute-start(bf16[256,1024]{1,0:T(8,128)(2,1)S(1)} %add_convert_fusion.3), channel_id=1, source_target_pairs={{0,2},{2,0},{4,6},{6,4},{8,10},{10,8},{12,14},{14,12},{1,3},{3,1},... | collective-permute-start | bytes 1572872 | tf_op jit(solution)/shard_map/ppermute | solution.py:206
  185.6 14.9 %collective-permute-start.15 = (bf16[256,1024]{1,0:T(8,128)(2,1)S(1)}, bf16[256,1024]{1,0:T(8,128)(2,1)S(1)}, u32[]{:S(2)}, u32[]{:S(2)}) collective-permute-start(bf16[256,1024]{1,0:T(8,128)(2,1)S(1)} %get-tuple-element.82), channel_id=1, source_target_pairs={{0,2},{2,0},{4,6},{6,4},{8,10},{10,8},{12,14},{14,12},{1,3},{3,1},... | collective-permute-start | bytes 1572872 | tf_op jit(solution)/shard_map/ppermute | solution.py:206
  186.5 15.6 %collective-permute-start.20 = (bf16[256,1024]{1,0:T(8,128)(2,1)S(1)}, bf16[256,1024]{1,0:T(8,128)(2,1)S(1)}, u32[]{:S(2)}, u32[]{:S(2)}) collective-permute-start(bf16[256,1024]{1,0:T(8,128)(2,1)S(1)} %add_convert_fusion.7), channel_id=1, source_target_pairs={{0,4},{2,6},{12,8},{14,10},{1,5},{3,7},{13,9},{15,11},{16,20},{18,... | collective-permute-start | bytes 1572872 | tf_op jit(solution)/shard_map/ppermute | solution.py:195
  188.0 14.7 %collective-permute-start.18 = (bf16[256,1024]{1,0:T(8,128)(2,1)S(1)}, bf16[256,1024]{1,0:T(8,128)(2,1)S(1)}, u32[]{:S(2)}, u32[]{:S(2)}) collective-permute-start(bf16[256,1024]{1,0:T(8,128)(2,1)S(1)} %add_convert_fusion.7), channel_id=1, source_target_pairs={{4,8},{6,10},{8,4},{10,6},{5,9},{7,11},{9,5},{11,7},{20,24},{22,26... | collective-permute-start | bytes 1572872 | tf_op jit(solution)/shard_map/ppermute | solution.py:195
  191.9 23.5 %collective-permute-start.30 = (bf16[256,1024]{1,0:T(8,128)(2,1)S(1)}, bf16[256,1024]{1,0:T(8,128)(2,1)S(1)}, u32[]{:S(2)}, u32[]{:S(2)}) collective-permute-start(bf16[256,1024]{1,0:T(8,128)(2,1)S(1)} %add_convert_fusion.2), channel_id=1, source_target_pairs={{0,4},{2,6},{12,8},{14,10},{1,5},{3,7},{13,9},{15,11},{16,20},{18,... | collective-permute-start | bytes 1572872 | tf_op jit(solution)/shard_map/ppermute | solution.py:195
  193.2 23.9 %collective-permute-start.28 = (bf16[256,1024]{1,0:T(8,128)(2,1)S(1)}, bf16[256,1024]{1,0:T(8,128)(2,1)S(1)}, u32[]{:S(2)}, u32[]{:S(2)}) collective-permute-start(bf16[256,1024]{1,0:T(8,128)(2,1)S(1)} %add_convert_fusion.2), channel_id=1, source_target_pairs={{4,8},{6,10},{8,4},{10,6},{5,9},{7,11},{9,5},{11,7},{20,24},{22,26... | collective-permute-start | bytes 1572872 | tf_op jit(solution)/shard_map/ppermute | solution.py:195
  200.5 14.9 %collective-permute-start.25 = (bf16[256,1024]{1,0:T(8,128)(2,1)S(1)}, bf16[256,1024]{1,0:T(8,128)(2,1)S(1)}, u32[]{:S(2)}, u32[]{:S(2)}) collective-permute-start(bf16[256,1024]{1,0:T(8,128)(2,1)S(1)} %get-tuple-element.91), channel_id=1, source_target_pairs={{0,2},{2,0},{4,6},{6,4},{8,10},{10,8},{12,14},{14,12},{1,3},{3,1},... | collective-permute-start | bytes 1572872 | tf_op jit(solution)/shard_map/ppermute | solution.py:206
  202.0 24.6 %collective-permute-start.16 = (bf16[256,1024]{1,0:T(8,128)(2,1)S(1)}, bf16[256,1024]{1,0:T(8,128)(2,1)S(1)}, u32[]{:S(2)}, u32[]{:S(2)}) collective-permute-start(bf16[256,1024]{1,0:T(8,128)(2,1)S(1)} %get-tuple-element.83), channel_id=1, source_target_pairs={{0,2},{2,0},{4,6},{6,4},{8,10},{10,8},{12,14},{14,12},{1,3},{3,1},... | collective-permute-start | bytes 1572872 | tf_op jit(solution)/shard_map/ppermute | solution.py:206
  202.8 29.0 %collective-permute-start.21 = (bf16[256,1024]{1,0:T(8,128)(2,1)S(1)}, bf16[256,1024]{1,0:T(8,128)(2,1)S(1)}, u32[]{:S(2)}, u32[]{:S(2)}) collective-permute-start(bf16[256,1024]{1,0:T(8,128)(2,1)S(1)} %add_convert_fusion.5), channel_id=1, source_target_pairs={{4,8},{6,10},{8,4},{10,6},{5,9},{7,11},{9,5},{11,7},{20,24},{22,26... | collective-permute-start | bytes 1572872 | tf_op jit(solution)/shard_map/ppermute | solution.py:195
  215.4 16.3 %collective-permute-start.19 = (bf16[256,1024]{1,0:T(8,128)(2,1)S(1)}, bf16[256,1024]{1,0:T(8,128)(2,1)S(1)}, u32[]{:S(2)}, u32[]{:S(2)}) collective-permute-start(bf16[256,1024]{1,0:T(8,128)(2,1)S(1)} %add_convert_fusion.6), channel_id=1, source_target_pairs={{0,4},{2,6},{4,0},{6,2},{8,12},{10,14},{12,8},{14,10},{1,5},{3,7},... | collective-permute-start | bytes 1572872 | tf_op jit(solution)/shard_map/ppermute | solution.py:195
  215.4 19.2 %collective-permute-start.26 = (bf16[256,1024]{1,0:T(8,128)(2,1)S(1)}, bf16[256,1024]{1,0:T(8,128)(2,1)S(1)}, u32[]{:S(2)}, u32[]{:S(2)}) collective-permute-start(bf16[256,1024]{1,0:T(8,128)(2,1)S(1)} %add_convert_fusion.4), channel_id=1, source_target_pairs={{0,2},{2,0},{4,6},{6,4},{8,10},{10,8},{12,14},{14,12},{1,3},{3,1},... | collective-permute-start | bytes 1572872 | tf_op jit(solution)/shard_map/ppermute | solution.py:206
  217.1 17.5 %collective-permute-start.31 = (bf16[256,1024]{1,0:T(8,128)(2,1)S(1)}, bf16[256,1024]{1,0:T(8,128)(2,1)S(1)}, u32[]{:S(2)}, u32[]{:S(2)}) collective-permute-start(bf16[256,1024]{1,0:T(8,128)(2,1)S(1)} %add_convert_fusion), channel_id=1, source_target_pairs={{4,8},{6,10},{8,4},{10,6},{5,9},{7,11},{9,5},{11,7},{20,24},{22,26... | collective-permute-start | bytes 1572872 | tf_op jit(solution)/shard_map/ppermute | solution.py:195
  226.6 9.2 %collective-permute-start.29 = (bf16[256,1024]{1,0:T(8,128)(2,1)S(1)}, bf16[256,1024]{1,0:T(8,128)(2,1)S(1)}, u32[]{:S(2)}, u32[]{:S(2)}) collective-permute-start(bf16[256,1024]{1,0:T(8,128)(2,1)S(1)} %add_convert_fusion.1), channel_id=1, source_target_pairs={{0,4},{2,6},{4,0},{6,2},{8,12},{10,14},{12,8},{14,10},{1,5},{3,7},... | collective-permute-start | bytes 1572872 | tf_op jit(solution)/shard_map/ppermute | solution.py:195
  (16 other events, 131.6 us)
where the time goes:
time: 239 us; the launch traced here: 238 us
  Pallas kernels  101 us (42%)
  waiting for transfers between devices  53.3 us (22%)
  starting transfers between devices  48.9 us (20%)
  local copies, waits for them, and re-layouts  28.1 us (12%)
  other arithmetic  5.49 us (2%)
    pallas_call x5, Pallas kernels, accumulate(): pl.pallas_call(functools.partial(accumulate_kernel, depths, pairs, width,...  50.3 us
    ppermute x11, waiting for transfers between devices, across(): return lax.ppermute(block, 'chan', [(c, c ^ 1) for c in range(count)])  33.3 us
    ppermute x19, starting transfers between devices, along_line(): lax.ppermute(block, 'chan', [(2 * a + y, 2 * b + y) for a, b in pairs for...  31.7 us
    pallas_call x10, Pallas kernels, pieces(): pl.pallas_call(functools.partial(pieces_kernel, count), grid_spec=pltpu.P...  31.4 us
    unnamed x34, local copies, waits for them, and re-layouts  25.5 us
    ppermute x19, waiting for transfers between devices, along_line(): lax.ppermute(block, 'chan', [(2 * a + y, 2 * b + y) for a, b in pairs for...  18.4 us
    ppermute x11, starting transfers between devices, across(): return lax.ppermute(block, 'chan', [(c, c ^ 1) for c in range(count)])  13.5 us
    pallas_call x1, Pallas kernels, mix(): pl.pallas_call(mix_kernel, grid=(rows // blk,), in_specs=[pl.BlockSpec((3...  13.1 us
  transfers between devices with their start and end apart: 32, of which 12 were waited for; matrix products, arithmetic and copies ran while one was open for 4% of the time, Pallas kernels for 31%

commit v1 on v0

--- a/solution.py
+++ b/solution.py
@@ -111,7 +111,7 @@
         ),
         out_shape=out_shape,
         input_output_aliases=aliases,
-        compiler_params=pltpu.CompilerParams(vmem_limit_bytes=26 * 1024 * 1024),
+        compiler_params=pltpu.CompilerParams(vmem_limit_bytes=VMEM_LIMIT),
         cost_estimate=pl.CostEstimate(
             flops=rows * sum(depths) * chans,
             bytes_accessed=6 * sum(depths) * chans,
@@ -227,18 +227,17 @@
     next_over = across(next_one, own_over, held[1])
     second_out = along_line(after(middle, held[1]), OUTWARD)
     second_mid = along_line(after(next_one, held[1]), MIDDLE)
-    held = accumulate([own_over, next_one], [me ^ 1, me ^ 2], gain, in_weight, held)
+    square, *params = lax.optimization_barrier((held[1], *params))
+    held = accumulate([own_over, next_one], [me ^ 1, me ^ 2], gain, in_weight, (held[0], square))
     second = jnp.where(at_end, second_out, second_mid)
     second_over = across(second, next_over, held[1])
     third_out = along_line(after(second_mid, second_out, held[1]), OUTWARD)
     rest_mid = along_line(after(own_over[:, half:], second_mid, held[1]), MIDDLE)
     held = accumulate([next_over, second], [me ^ 3, me ^ 4], gain, in_weight, held)
-    third = jnp.where(at_end, third_out, middle)
-    third_over = across(third[:, :half], second_over, held[1])
+    third_over = across(jnp.where(at_end, third_out[:, :half], middle[:, :half]), second_over, held[1])
     rest_out = along_line(after(second_over[:, half:], held[1]), OUTWARD)
-    square, *params = lax.optimization_barrier((held[1], *params))
-    held = (held[0], square)
-    held = accumulate([second_over, third], [me ^ 5, me ^ 6], gain, in_weight, held)
+    third = (third_out, middle)
+    held = accumulate([second_over, third], [me ^ 5, me ^ 6], gain, in_weight, held, use_first=at_end)
     last = [third_over, (rest_out, rest_mid)]
     place = (me ^ 7) * 2
     return accumulate(last, [place, place + 1], gain, in_weight, held, last=True, use_first=at_end), params
@@ -267,7 +266,7 @@
     second_send = [second_send_0, narrow(total(second_send_1, rest_in))]
     second_over = [across(second_send[h], third_over) for h in both]
     halves = (upper, lower)
-    later = [make(halves[h], [keep(2), send(1)], third_1) for h in both]
+    later = [make(halves[h], [keep(2), send(1)], (third_over, second_send[1])[h]) for h in both]
     second = [narrow(total(later[h][0], second_over[h], third_in[h])) for h in both]
     second_in = [along_line(second[h], INWARD) for h in both]
     second_mid = [along_line(second[h], MIDDLE) for h in both]
@@ -388,7 +387,7 @@
             pltpu.VMEM((blk, groups, LANES), jnp.float32),
             pltpu.VMEM((poles, groups, LANES), jnp.float32),
         ],
-        compiler_params=pltpu.CompilerParams(vmem_limit_bytes=26 * 1024 * 1024),
+        compiler_params=pltpu.CompilerParams(vmem_limit_bytes=VMEM_LIMIT),
         cost_estimate=pl.CostEstimate(
             flops=110 * rows * groups * LANES, bytes_accessed=20 * rows * groups * LANES, transcendentals=0
         ),
@@ -444,7 +443,7 @@
             pltpu.VMEM((poles, groups, LANES), jnp.float32),
             pltpu.VMEM((blk, groups, LANES), jnp.float32),
         ],
-        compiler_params=pltpu.CompilerParams(vmem_limit_bytes=26 * 1024 * 1024),
+        compiler_params=pltpu.CompilerParams(vmem_limit_bytes=VMEM_LIMIT),
         cost_estimate=pl.CostEstimate(
             flops=40 * rows * groups * LANES, bytes_accessed=80 * rows * groups * LANES, transcendentals=0
         ),

time: 239 us -> 237 us (level)
  local copies, waits for them, and re-layouts: 28.1 us -> 5.27 us
  Pallas kernels: 101 us -> 117 us
  starting transfers between devices: 48.9 us -> 55.3 us
    unnamed x34 -> x22, local copies, waits for them, and re-layouts: 25.5 us -> 2.71 us
    ppermute x11, waiting for transfers between devices: 33.3 us -> 11.9 us  [across(): return lax.ppermute(block, 'chan', [(c, c ^ 1) for c in range(count)])]
    ppermute x19, waiting for transfers between devices: 18.4 us -> 38.4 us  [along_line(): lax.ppermute(block, 'chan', [(2 * a + y, 2 * b + y) for a, b in pairs for...]
    pallas_call x5, Pallas kernels: 50.3 us -> 64.7 us  [accumulate(): pl.pallas_call(functools.partial(accumulate_kernel, depths, pairs, width,...]
    ppermute x19, starting transfers between devices: 31.7 us -> 36.7 us  [along_line(): lax.ppermute(block, 'chan', [(2 * a + y, 2 * b + y) for a, b in pairs for...]
  transfers between devices with their start and end apart: 32 -> 32, of which waited for: 12 -> 15; matrix products, arithmetic and copies ran while one was open for 4% -> 4% of each run, Pallas kernels for 31% -> 34%
where the time goes in v1:
time: 237 us; the launch traced here: 236 us
  Pallas kernels  117 us (49%)
  starting transfers between devices  55.3 us (23%)
  waiting for transfers between devices  52 us (22%)
  other arithmetic  6.01 us (3%)
  local copies, waits for them, and re-layouts  5.27 us (2%)
    pallas_call x5, Pallas kernels, accumulate(): pl.pallas_call(functools.partial(accumulate_kernel, depths, pairs, width,...  64.7 us
    ppermute x19, waiting for transfers between devices, along_line(): lax.ppermute(block, 'chan', [(2 * a + y, 2 * b + y) for a, b in pairs for...  38.4 us
    ppermute x19, starting transfers between devices, along_line(): lax.ppermute(block, 'chan', [(2 * a + y, 2 * b + y) for a, b in pairs for...  36.7 us
    pallas_call x10, Pallas kernels, pieces(): pl.pallas_call(functools.partial(pieces_kernel, count), grid_spec=pltpu.P...  31.4 us
    ppermute x11, starting transfers between devices, across(): return lax.ppermute(block, 'chan', [(c, c ^ 1) for c in range(count)])  15.1 us
    pallas_call x1, Pallas kernels, mix(): pl.pallas_call(mix_kernel, grid=(rows // blk,), in_specs=[pl.BlockSpec((3...  14.1 us
    ppermute x11, waiting for transfers between devices, across(): return lax.ppermute(block, 'chan', [(c, c ^ 1) for c in range(count)])  11.9 us
  transfers between devices with their start and end apart: 32, of which 15 were waited for; matrix products, arithmetic and copies ran while one was open for 4% of the time, Pallas kernels for 34%

profile of v1, /device:TPU:0, one launch (start us, length us, event | category | flops | bytes accessed | tf_op | source)
XLA Modules:
  0.0 235.8 jit_solution(10506825964042576496)
XLA Ops:
  0.0 3.0 %collective-permute-start = (bf16[512,1024]{1,0:T(8,128)(2,1)}, bf16[512,1024]{1,0:T(8,128)(2,1)}, u32[]{:S(2)}, u32[]{:S(2)}) collective-permute-start(bf16[512,1024]{1,0:T(8,128)(2,1)} %refs_0_.1), channel_id=1, source_target_pairs={{0,4},{2,6},{4,0},{6,2},{8,12},{10,14},{12,8},{14,10},{1,5},{3,7},... | collective-permute-start | bytes 3145736 | tf_op jit(solution)/shard_map/ppermute | solution.py:195
  7.4 8.9 %accumulate.5 = (f32[3,512,1024]{2,1,0:T(8,128)}, f32[512,128]{1,0:T(8,128)S(1)}) custom-call(s32[1]{0:T(128)} %bitcast.place_ref, bf16[512,1024]{1,0:T(8,128)(2,1)S(1)} %copy-done, f32[8,1,1024]{2,1,0:T(1,128)S(1)} %bitcast.18, bf16[3,8192,1024]{2,1,0:T(8,128)(2,1)} %refs_6_.3), custom_call_target="tpu_custom_call" | custom-call | flops 536870912 | bytes 6291456 | tf_op jit(solution)/shard_map/accumulate/pallas_call | solution.py:103
  16.2 10.3 %collective-permute-done.refs_1_ = bf16[512,1024]{1,0:T(8,128)(2,1)} collective-permute-done((bf16[512,1024]{1,0:T(8,128)(2,1)}, bf16[512,1024]{1,0:T(8,128)(2,1)}, u32[]{:S(2)}, u32[]{:S(2)}) %collective-permute-start) | collective-permute-done | bytes 1048608 | tf_op jit(solution)/shard_map/ppermute | solution.py:195
  32.6 14.8 %accumulate.6 = (f32[3,512,1024]{2,1,0:T(8,128)}, f32[512,128]{1,0:T(8,128)S(1)}) custom-call(s32[2]{0:T(128)S(1)} %pad_add_fusion.place_ref, bf16[512,1024]{1,0:T(8,128)(2,1)S(1)} %collective-permute-done.4.refs_0_, bf16[512,1024]{1,0:T(8,128)(2,1)} %collective-permute-done.refs_1_, ...), custom_call_target="tpu_custom_call", output_to_operand_aliasing={{0}: (7, {}), {1}: (8, {})} | custom-call | flops 1073741824 | bytes 12582912 | tf_op jit(solution)/shard_map/accumulate/pallas_call | solution.py:103
  47.4 10.5 %collective-permute-done.3 = bf16[512,1024]{1,0:T(8,128)(2,1)} collective-permute-done((bf16[512,1024]{1,0:T(8,128)(2,1)S(1)}, bf16[512,1024]{1,0:T(8,128)(2,1)}, u32[]{:S(2)}, u32[]{:S(2)}) %collective-permute-start.3) | collective-permute-done | bytes 1048608 | tf_op jit(solution)/shard_map/ppermute | solution.py:195
  63.7 14.8 %accumulate.7 = (f32[3,512,1024]{2,1,0:T(8,128)}, f32[512,128]{1,0:T(8,128)S(1)}) custom-call(s32[2]{0:T(128)S(1)} %pad_add_fusion.1.place_ref, bf16[512,1024]{1,0:T(8,128)(2,1)} %collective-permute-done.6.refs_0_, bf16[512,1024]{1,0:T(8,128)(2,1)S(1)} %broadcast_select_fusion.refs_1_, ...), custom_call_target="tpu_custom_call", output_to_operand_aliasing={{0}: (7, {}), {1}: (8, {})} | custom-call | flops 1073741824 | bytes 12582912 | tf_op jit(solution)/shard_map/accumulate/pallas_call | solution.py:103
  78.5 3.7 %collective-permute-done.7.refs_0_ = bf16[512,1024]{1,0:T(8,128)(2,1)} collective-permute-done((bf16[512,1024]{1,0:T(8,128)(2,1)S(1)}, bf16[512,1024]{1,0:T(8,128)(2,1)}, u32[]{:S(2)}, u32[]{:S(2)}) %collective-permute-start.7) | collective-permute-done | bytes 1048608 | tf_op jit(solution)/shard_map/ppermute | solution.py:206
  89.4 15.1 %accumulate.8 = (f32[3,512,1024]{2,1,0:T(8,128)}, f32[512,128]{1,0:T(8,128)S(1)}) custom-call(s32[3]{0:T(128)S(1)} %add_add_fusion.1.place_ref, bf16[512,1024]{1,0:T(8,128)(2,1)} %collective-permute-done.7.refs_0_, bf16[512,1024]{1,0:T(8,128)(2,1)} %collective-permute-done.5.refs_1_, ...), custom_call_target="tpu_custom_call", output_to_operand_aliasing={{0}: (8, {}), {1}: (9, {})} | custom-call | flops 1073741824 | bytes 12582912 | tf_op jit(solution)/shard_map/accumulate/pallas_call | solution.py:103
  104.6 11.1 %accumulate.9 = (f32[3,512,1024]{2,1,0:T(8,128)}, f32[512,128]{1,0:T(8,128)S(1)}, f32[3,8,1024]{2,1,0:T(8,128)S(1)}) custom-call(s32[3]{0:T(128)S(1)} %add_add_fusion.place_ref, bf16[512,512]{1,0:T(8,128)(2,1)S(1)} %collective-permute-done.8.refs_0_, ...), custom_call_target="tpu_custom_call", output_to_operand_aliasing={{0}: (8, {}), {1}: (9, {})} | custom-call | flops 536870912 | bytes 6291456 | tf_op jit(solution)/shard_map/accumulate/pallas_call | solution.py:103
  117.9 14.1 %mix.1 = (f32[512,8,128]{2,1,0:T(8,128)S(1)}, f32[512,8,128]{2,1,0:T(8,128)S(1)}, f32[16,8,128]{2,1,0:T(8,128)S(1)}) custom-call(f32[3,512,1024]{2,1,0:T(8,128)} %get-tuple-element.67.acc_ref, f32[512,128]{1,0:T(8,128)S(1)} %get-tuple-element.68.rms_ref, f32[3,8,1024]{2,1,0:T(8,128)S(1)} %collective-permute-done.11.rim_ref, f32[3,7,8,128]{3,2,1,0:T(8,128)S(1)} %copy-done.5, ...), custom_call_target="tpu_custom_call" | custom-call | flops 57671680 | bytes 10485760 | tf_op jit(solution)/shard_map/mix/pallas_call | solution.py:367
  132.1 2.3 collective-permute-start.12
  135.2 2.3 carry.2.gated_ref
  137.6 2.3 pieces.10.refs_0_
  139.9 2.4 carry.3.gated_ref
  142.2 2.3 pieces.11.refs_0_
  144.5 4.8 %collective-permute-start.23 = (bf16[256,1024]{1,0:T(8,128)(2,1)S(1)}, bf16[256,1024]{1,0:T(8,128)(2,1)S(1)}, u32[]{:S(2)}, u32[]{:S(2)}) collective-permute-start(bf16[256,1024]{1,0:T(8,128)(2,1)S(1)} %pieces.11.refs_0_), channel_id=1, source_target_pairs={{0,4},{2,6},{12,8},{14,10},{1,5},{3,7},{13,9},{15,11},{16,20},{18,... | collective-permute-start | bytes 1572872 | tf_op jit(solution)/shard_map/ppermute | solution.py:195
  151.0 3.7 %pieces.12 = (bf16[256,1024]{1,0:T(8,128)(2,1)S(1)}, f32[256,1024]{1,0:T(8,128)S(1)}) custom-call(s32[2]{0:T(128)S(1)} %pad_add_fusion.2.place_ref, bf16[256,1024]{1,0:T(8,128)(2,1)S(1)} %carry.2.gated_ref, bf16[1024,8192]{1,0:T(8,128)(2,1)} %w_ref.19, bf16[256,1024]{1,0:T(8,128)(2,1)S(1)} %pieces.11.refs_0_), custom_call_target="tpu_custom_call" | custom-call | flops 2000000 | bytes 200000 | tf_op jit(solution)/shard_map/pieces/pallas_call | solution.py:143
  154.7 3.7 %pieces.18 = (bf16[256,1024]{1,0:T(8,128)(2,1)S(1)}, bf16[256,1024]{1,0:T(8,128)(2,1)S(1)}) custom-call(s32[2]{0:T(128)S(1)} %pad_add_fusion.2.place_ref, bf16[256,1024]{1,0:T(8,128)(2,1)S(1)} %carry.3.gated_ref, bf16[1024,8192]{1,0:T(8,128)(2,1)} %w_ref.19, bf16[256,1024]{1,0:T(8,128)(2,1)S(1)} %get-tuple-element.78.refs_0_), custom_call_target="tpu_custom_call" | custom-call | flops 2000000 | bytes 200000 | tf_op jit(solution)/shard_map/pieces/pallas_call | solution.py:143
  165.8 4.9 %collective-permute-start.17 = (bf16[256,1024]{1,0:T(8,128)(2,1)S(1)}, bf16[256,1024]{1,0:T(8,128)(2,1)S(1)}, u32[]{:S(2)}, u32[]{:S(2)}) collective-permute-start(bf16[256,1024]{1,0:T(8,128)(2,1)S(1)} %add_convert_fusion.8), channel_id=1, source_target_pairs={{0,4},{2,6},{12,8},{14,10},{1,5},{3,7},{13,9},{15,11},{16,20},{18,... | collective-permute-start | bytes 1572872 | tf_op jit(solution)/shard_map/ppermute | solution.py:195
  171.3 3.7 %pieces.19 = (f32[256,1024]{1,0:T(8,128)S(1)}, bf16[256,1024]{1,0:T(8,128)(2,1)S(1)}) custom-call(s32[2]{0:T(128)S(1)} %pad_add_fusion.4.place_ref, bf16[256,1024]{1,0:T(8,128)(2,1)S(1)} %carry.3.gated_ref, bf16[1024,8192]{1,0:T(8,128)(2,1)} %w_ref.19, bf16[256,1024]{1,0:T(8,128)(2,1)S(1)} %add_convert_fusion.3.refs_0_), custom_call_target="tpu_custom_call" | custom-call | flops 2000000 | bytes 200000 | tf_op jit(solution)/shard_map/pieces/pallas_call | solution.py:143
  175.0 3.7 %pieces.15 = (f32[256,1024]{1,0:T(8,128)S(1)}, bf16[256,1024]{1,0:T(8,128)(2,1)S(1)}) custom-call(s32[2]{0:T(128)S(1)} %pad_add_fusion.4.place_ref, bf16[256,1024]{1,0:T(8,128)(2,1)S(1)} %carry.2.gated_ref, bf16[1024,8192]{1,0:T(8,128)(2,1)} %w_ref.19, bf16[256,1024]{1,0:T(8,128)(2,1)S(1)} %collective-permute-done.13.refs_0_), custom_call_target="tpu_custom_call" | custom-call | flops 2000000 | bytes 200000 | tf_op jit(solution)/shard_map/pieces/pallas_call | solution.py:143
  178.7 3.7 %pieces.17 = (f32[256,1024]{1,0:T(8,128)S(1)}, bf16[256,1024]{1,0:T(8,128)(2,1)S(1)}) custom-call(s32[2]{0:T(128)S(1)} %pad_add_fusion.3.place_ref, bf16[256,1024]{1,0:T(8,128)(2,1)S(1)} %carry.3.gated_ref, bf16[1024,8192]{1,0:T(8,128)(2,1)} %w_ref.19, bf16[256,1024]{1,0:T(8,128)(2,1)S(1)} %collective-permute-done.13.refs_0_), custom_call_target="tpu_custom_call" | custom-call | flops 2000000 | bytes 200000 | tf_op jit(solution)/shard_map/pieces/pallas_call | solution.py:143
  182.3 3.7 %pieces.14 = (f32[256,1024]{1,0:T(8,128)S(1)}, bf16[256,1024]{1,0:T(8,128)(2,1)S(1)}) custom-call(s32[2]{0:T(128)S(1)} %pad_add_fusion.3.place_ref, bf16[256,1024]{1,0:T(8,128)(2,1)S(1)} %carry.2.gated_ref, bf16[1024,8192]{1,0:T(8,128)(2,1)} %w_ref.19, bf16[256,1024]{1,0:T(8,128)(2,1)S(1)} %collective-permute-done.13.refs_0_), custom_call_target="tpu_custom_call" | custom-call | flops 2000000 | bytes 200000 | tf_op jit(solution)/shard_map/pieces/pallas_call | solution.py:143
  190.4 3.6 %collective-permute-start.20 = (bf16[256,1024]{1,0:T(8,128)(2,1)S(1)}, bf16[256,1024]{1,0:T(8,128)(2,1)S(1)}, u32[]{:S(2)}, u32[]{:S(2)}) collective-permute-start(bf16[256,1024]{1,0:T(8,128)(2,1)S(1)} %add_convert_fusion.7), channel_id=1, source_target_pairs={{0,4},{2,6},{12,8},{14,10},{1,5},{3,7},{13,9},{15,11},{16,20},{18,... | collective-permute-start | bytes 1572872 | tf_op jit(solution)/shard_map/ppermute | solution.py:195
  194.7 5.3 %collective-permute-done.30 = bf16[256,1024]{1,0:T(8,128)(2,1)S(1)} collective-permute-done((bf16[256,1024]{1,0:T(8,128)(2,1)S(1)}, bf16[256,1024]{1,0:T(8,128)(2,1)S(1)}, u32[]{:S(2)}, u32[]{:S(2)}) %collective-permute-start.30) | collective-permute-done | bytes 524320 | tf_op jit(solution)/shard_map/ppermute | solution.py:195
  203.7 3.8 %collective-permute-start.29 = (bf16[256,1024]{1,0:T(8,128)(2,1)S(1)}, bf16[256,1024]{1,0:T(8,128)(2,1)S(1)}, u32[]{:S(2)}, u32[]{:S(2)}) collective-permute-start(bf16[256,1024]{1,0:T(8,128)(2,1)S(1)} %add_convert_fusion.1), channel_id=1, source_target_pairs={{0,4},{2,6},{4,0},{6,2},{8,12},{10,14},{12,8},{14,10},{1,5},{3,7},... | collective-permute-start | bytes 1572872 | tf_op jit(solution)/shard_map/ppermute | solution.py:195
  207.5 3.7 %collective-permute-done.20 = bf16[256,1024]{1,0:T(8,128)(2,1)S(1)} collective-permute-done((bf16[256,1024]{1,0:T(8,128)(2,1)S(1)}, bf16[256,1024]{1,0:T(8,128)(2,1)S(1)}, u32[]{:S(2)}, u32[]{:S(2)}) %collective-permute-start.20) | collective-permute-done | bytes 524320 | tf_op jit(solution)/shard_map/ppermute | solution.py:195
  215.1 3.7 %collective-permute-start.19 = (bf16[256,1024]{1,0:T(8,128)(2,1)S(1)}, bf16[256,1024]{1,0:T(8,128)(2,1)S(1)}, u32[]{:S(2)}, u32[]{:S(2)}) collective-permute-start(bf16[256,1024]{1,0:T(8,128)(2,1)S(1)} %add_convert_fusion.6), channel_id=1, source_target_pairs={{0,4},{2,6},{4,0},{6,2},{8,12},{10,14},{12,8},{14,10},{1,5},{3,7},... | collective-permute-start | bytes 1572872 | tf_op jit(solution)/shard_map/ppermute | solution.py:195
  220.0 2.3 pieces.13
  222.3 2.4 %pieces.16 = f32[256,1024]{1,0:T(8,128)S(1)} custom-call(s32[1]{0:T(128)} %bitcast.place_ref, bf16[256,1024]{1,0:T(8,128)(2,1)S(1)} %carry.3.gated_ref, bf16[1024,8192]{1,0:T(8,128)(2,1)} %w_ref.19, bf16[256,1024]{1,0:T(8,128)(2,1)S(1)} %collective-permute-done.14.refs_0_), custom_call_target="tpu_custom_call" | custom-call | flops 1000000 | bytes 100000 | tf_op jit(solution)/shard_map/pieces/pallas_call | solution.py:143
  226.1 4.7 %collective-permute-done.19.refs_2_ = bf16[256,1024]{1,0:T(8,128)(2,1)S(1)} collective-permute-done((bf16[256,1024]{1,0:T(8,128)(2,1)S(1)}, bf16[256,1024]{1,0:T(8,128)(2,1)S(1)}, u32[]{:S(2)}, u32[]{:S(2)}) %collective-permute-start.19) | collective-permute-done | bytes 524320 | tf_op jit(solution)/shard_map/ppermute | solution.py:195
  230.8 3.2 %collective-permute-done.16.refs_1_ = bf16[256,1024]{1,0:T(8,128)(2,1)S(1)} collective-permute-done((bf16[256,1024]{1,0:T(8,128)(2,1)S(1)}, bf16[256,1024]{1,0:T(8,128)(2,1)S(1)}, u32[]{:S(2)}, u32[]{:S(2)}) %collective-permute-start.16) | collective-permute-done | bytes 524320 | tf_op jit(solution)/shard_map/ppermute | solution.py:206
  (95 shorter events, 53.0 us)
Async XLA Ops:
  0.0 26.5 %collective-permute-start = (bf16[512,1024]{1,0:T(8,128)(2,1)}, bf16[512,1024]{1,0:T(8,128)(2,1)}, u32[]{:S(2)}, u32[]{:S(2)}) collective-permute-start(bf16[512,1024]{1,0:T(8,128)(2,1)} %refs_0_.1), channel_id=1, source_target_pairs={{0,4},{2,6},{4,0},{6,2},{8,12},{10,14},{12,8},{14,10},{1,5},{3,7},... | collective-permute-start | bytes 3145736 | tf_op jit(solution)/shard_map/ppermute | solution.py:195
  3.0 23.5 %collective-permute-start.2 = (bf16[512,1024]{1,0:T(8,128)(2,1)}, bf16[512,1024]{1,0:T(8,128)(2,1)S(1)}, u32[]{:S(2)}, u32[]{:S(2)}) collective-permute-start(bf16[512,1024]{1,0:T(8,128)(2,1)} %refs_0_.1), channel_id=1, source_target_pairs={{4,8},{6,10},{8,4},{10,6},{5,9},{7,11},{9,5},{11,7},{20,24},{22,26... | collective-permute-start | bytes 3145736 | tf_op jit(solution)/shard_map/ppermute | solution.py:195
  3.7 25.7 %collective-permute-start.4 = (bf16[512,1024]{1,0:T(8,128)(2,1)}, bf16[512,1024]{1,0:T(8,128)(2,1)S(1)}, u32[]{:S(2)}, u32[]{:S(2)}) collective-permute-start(bf16[512,1024]{1,0:T(8,128)(2,1)} %refs_0_.1), channel_id=1, source_target_pairs={{0,2},{2,0},{4,6},{6,4},{8,10},{10,8},{12,14},{14,12},{1,3},{3,1},... | collective-permute-start | bytes 3145736 | tf_op jit(solution)/shard_map/ppermute | solution.py:206
  26.5 20.9 %collective-permute-start.1 = (bf16[512,1024]{1,0:T(8,128)(2,1)}, bf16[512,1024]{1,0:T(8,128)(2,1)}, u32[]{:S(2)}, u32[]{:S(2)}) collective-permute-start(bf16[512,1024]{1,0:T(8,128)(2,1)} %collective-permute-done.refs_1_), channel_id=1, source_target_pairs={{4,8},{6,10},{8,4},{10,6},{5,9},{7,11},{9,5},{11,7},{20,24},{22,26... | collective-permute-start | bytes 3145736 | tf_op jit(solution)/shard_map/ppermute | solution.py:195
  28.1 29.7 %collective-permute-start.3 = (bf16[512,1024]{1,0:T(8,128)(2,1)S(1)}, bf16[512,1024]{1,0:T(8,128)(2,1)}, u32[]{:S(2)}, u32[]{:S(2)}) collective-permute-start(bf16[512,1024]{1,0:T(8,128)(2,1)S(1)} %collective-permute-done.2.refs_2_), channel_id=1, source_target_pairs={{4,0},{6,2},{8,12},{10,14},{5,1},{7,3},{9,13},{11,15},{20,16},{22,... | collective-permute-start | bytes 3145736 | tf_op jit(solution)/shard_map/ppermute | solution.py:195
  29.4 29.8 %collective-permute-start.6 = (bf16[512,1024]{1,0:T(8,128)(2,1)}, bf16[512,1024]{1,0:T(8,128)(2,1)}, u32[]{:S(2)}, u32[]{:S(2)}) collective-permute-start(bf16[512,1024]{1,0:T(8,128)(2,1)} %collective-permute-done.refs_1_), channel_id=1, source_target_pairs={{0,2},{2,0},{4,6},{6,4},{8,10},{10,8},{12,14},{14,12},{1,3},{3,1},... | collective-permute-start | bytes 3145736 | tf_op jit(solution)/shard_map/ppermute | solution.py:206
  59.2 23.0 %collective-permute-start.7 = (bf16[512,1024]{1,0:T(8,128)(2,1)S(1)}, bf16[512,1024]{1,0:T(8,128)(2,1)}, u32[]{:S(2)}, u32[]{:S(2)}) collective-permute-start(bf16[512,1024]{1,0:T(8,128)(2,1)S(1)} %broadcast_select_fusion.refs_1_), channel_id=1, source_target_pairs={{0,2},{2,0},{4,6},{6,4},{8,10},{10,8},{12,14},{14,12},{1,3},{3,1},... | collective-permute-start | bytes 3145736 | tf_op jit(solution)/shard_map/ppermute | solution.py:206
  60.8 24.7 %collective-permute-start.5 = (bf16[512,1024]{1,0:T(8,128)(2,1)}, bf16[512,1024]{1,0:T(8,128)(2,1)}, u32[]{:S(2)}, u32[]{:S(2)}) collective-permute-start(bf16[512,1024]{1,0:T(8,128)(2,1)} %collective-permute-done.1), channel_id=1, source_target_pairs={{4,0},{6,2},{8,12},{10,14},{5,1},{7,3},{9,13},{11,15},{20,16},{22,... | collective-permute-start | bytes 3145736 | tf_op jit(solution)/shard_map/ppermute | solution.py:195
  63.0 41.5 %collective-permute-start.10 = (bf16[512,512]{1,0:T(8,128)(2,1)}, bf16[512,512]{1,0:T(8,128)(2,1)S(1)}, u32[]{:S(2)}, u32[]{:S(2)}) collective-permute-start(bf16[512,512]{1,0:T(8,128)(2,1)} %slice.27), channel_id=1, source_target_pairs={{4,8},{6,10},{8,4},{10,6},{5,9},{7,11},{9,5},{11,7},{20,24},{22,26... | collective-permute-start | bytes 1572872 | tf_op jit(solution)/shard_map/ppermute | solution.py:195
  87.4 17.2 %collective-permute-start.9 = (bf16[512,512]{1,0:T(8,128)(2,1)S(1)}, bf16[512,512]{1,0:T(8,128)(2,1)S(1)}, u32[]{:S(2)}, u32[]{:S(2)}) collective-permute-start(bf16[512,512]{1,0:T(8,128)(2,1)S(1)} %slice.26), channel_id=1, source_target_pairs={{4,0},{6,2},{8,12},{10,14},{5,1},{7,3},{9,13},{11,15},{20,16},{22,... | collective-permute-start | bytes 1572872 | tf_op jit(solution)/shard_map/ppermute | solution.py:195
  88.7 15.9 %collective-permute-start.8 = (bf16[512,512]{1,0:T(8,128)(2,1)}, bf16[512,512]{1,0:T(8,128)(2,1)S(1)}, u32[]{:S(2)}, u32[]{:S(2)}) collective-permute-start(bf16[512,512]{1,0:T(8,128)(2,1)} %slice_select_fusion), channel_id=1, source_target_pairs={{0,2},{2,0},{4,6},{6,4},{8,10},{10,8},{12,14},{14,12},{1,3},{3,1},... | collective-permute-start | bytes 1572872 | tf_op jit(solution)/shard_map/ppermute | solution.py:206
  115.7 2.2 collective-permute-start.11
  132.1 3.2 %collective-permute-start.12 = (f32[16,8,128]{2,1,0:T(8,128)S(1)}, f32[16,8,128]{2,1,0:T(8,128)S(1)}, u32[]{:S(2)}, u32[]{:S(2)}) collective-permute-start(f32[16,8,128]{2,1,0:T(8,128)S(1)} %get-tuple-element.76), channel_id=1, source_target_pairs={{0,1},{2,3},{4,5},{6,7},{8,9},{10,11},{12,13},{14,15},{16,17},{18,... | collective-permute-start | bytes 196616 | tf_op jit(solution)/shard_map/ppermute | solution.py:19
  144.5 16.8 %collective-permute-start.23 = (bf16[256,1024]{1,0:T(8,128)(2,1)S(1)}, bf16[256,1024]{1,0:T(8,128)(2,1)S(1)}, u32[]{:S(2)}, u32[]{:S(2)}) collective-permute-start(bf16[256,1024]{1,0:T(8,128)(2,1)S(1)} %pieces.11.refs_0_), channel_id=1, source_target_pairs={{0,4},{2,6},{12,8},{14,10},{1,5},{3,7},{13,9},{15,11},{16,20},{18,... | collective-permute-start | bytes 1572872 | tf_op jit(solution)/shard_map/ppermute | solution.py:195
  149.3 14.0 %collective-permute-start.13 = (bf16[256,1024]{1,0:T(8,128)(2,1)S(1)}, bf16[256,1024]{1,0:T(8,128)(2,1)S(1)}, u32[]{:S(2)}, u32[]{:S(2)}) collective-permute-start(bf16[256,1024]{1,0:T(8,128)(2,1)S(1)} %pieces.10.refs_0_), channel_id=1, source_target_pairs={{0,2},{2,0},{4,6},{6,4},{8,10},{10,8},{12,14},{14,12},{1,3},{3,1},... | collective-permute-start | bytes 1572872 | tf_op jit(solution)/shard_map/ppermute | solution.py:206
  158.4 27.6 %collective-permute-start.27 = (bf16[256,1024]{1,0:T(8,128)(2,1)S(1)}, bf16[256,1024]{1,0:T(8,128)(2,1)S(1)}, u32[]{:S(2)}, u32[]{:S(2)}) collective-permute-start(bf16[256,1024]{1,0:T(8,128)(2,1)S(1)} %get-tuple-element.94), channel_id=1, source_target_pairs={{0,4},{2,6},{12,8},{14,10},{1,5},{3,7},{13,9},{15,11},{16,20},{18,... | collective-permute-start | bytes 1572872 | tf_op jit(solution)/shard_map/ppermute | solution.py:195
  163.3 22.7 %collective-permute-start.24 = (bf16[256,1024]{1,0:T(8,128)(2,1)S(1)}, bf16[256,1024]{1,0:T(8,128)(2,1)S(1)}, u32[]{:S(2)}, u32[]{:S(2)}) collective-permute-start(bf16[256,1024]{1,0:T(8,128)(2,1)S(1)} %add_convert_fusion.3.refs_0_), channel_id=1, source_target_pairs={{0,2},{2,0},{4,6},{6,4},{8,10},{10,8},{12,14},{14,12},{1,3},{3,1},... | collective-permute-start | bytes 1572872 | tf_op jit(solution)/shard_map/ppermute | solution.py:206
  165.0 22.7 %collective-permute-start.22 = (bf16[256,1024]{1,0:T(8,128)(2,1)S(1)}, bf16[256,1024]{1,0:T(8,128)(2,1)S(1)}, u32[]{:S(2)}, u32[]{:S(2)}) collective-permute-start(bf16[256,1024]{1,0:T(8,128)(2,1)S(1)} %pieces.11.refs_0_), channel_id=1, source_target_pairs={{4,8},{6,10},{8,4},{10,6},{5,9},{7,11},{9,5},{11,7},{20,24},{22,26... | collective-permute-start | bytes 1572872 | tf_op jit(solution)/shard_map/ppermute | solution.py:195
  165.8 24.3 %collective-permute-start.17 = (bf16[256,1024]{1,0:T(8,128)(2,1)S(1)}, bf16[256,1024]{1,0:T(8,128)(2,1)S(1)}, u32[]{:S(2)}, u32[]{:S(2)}) collective-permute-start(bf16[256,1024]{1,0:T(8,128)(2,1)S(1)} %add_convert_fusion.8), channel_id=1, source_target_pairs={{0,4},{2,6},{12,8},{14,10},{1,5},{3,7},{13,9},{15,11},{16,20},{18,... | collective-permute-start | bytes 1572872 | tf_op jit(solution)/shard_map/ppermute | solution.py:195
  170.7 19.4 %collective-permute-start.14 = (bf16[256,1024]{1,0:T(8,128)(2,1)S(1)}, bf16[256,1024]{1,0:T(8,128)(2,1)S(1)}, u32[]{:S(2)}, u32[]{:S(2)}) collective-permute-start(bf16[256,1024]{1,0:T(8,128)(2,1)S(1)} %get-tuple-element.78.refs_0_), channel_id=1, source_target_pairs={{0,2},{2,0},{4,6},{6,4},{8,10},{10,8},{12,14},{14,12},{1,3},{3,1},... | collective-permute-start | bytes 1572872 | tf_op jit(solution)/shard_map/ppermute | solution.py:206
  186.3 13.7 %collective-permute-start.30 = (bf16[256,1024]{1,0:T(8,128)(2,1)S(1)}, bf16[256,1024]{1,0:T(8,128)(2,1)S(1)}, u32[]{:S(2)}, u32[]{:S(2)}) collective-permute-start(bf16[256,1024]{1,0:T(8,128)(2,1)S(1)} %add_convert_fusion.2), channel_id=1, source_target_pairs={{0,4},{2,6},{12,8},{14,10},{1,5},{3,7},{13,9},{15,11},{16,20},{18,... | collective-permute-start | bytes 1572872 | tf_op jit(solution)/shard_map/ppermute | solution.py:195
  187.8 13.8 %collective-permute-start.28 = (bf16[256,1024]{1,0:T(8,128)(2,1)S(1)}, bf16[256,1024]{1,0:T(8,128)(2,1)S(1)}, u32[]{:S(2)}, u32[]{:S(2)}) collective-permute-start(bf16[256,1024]{1,0:T(8,128)(2,1)S(1)} %add_convert_fusion.2), channel_id=1, source_target_pairs={{4,8},{6,10},{8,4},{10,6},{5,9},{7,11},{9,5},{11,7},{20,24},{22,26... | collective-permute-start | bytes 1572872 | tf_op jit(solution)/shard_map/ppermute | solution.py:195
  188.5 14.9 %collective-permute-start.25 = (bf16[256,1024]{1,0:T(8,128)(2,1)S(1)}, bf16[256,1024]{1,0:T(8,128)(2,1)S(1)}, u32[]{:S(2)}, u32[]{:S(2)}) collective-permute-start(bf16[256,1024]{1,0:T(8,128)(2,1)S(1)} %get-tuple-element.90), channel_id=1, source_target_pairs={{0,2},{2,0},{4,6},{6,4},{8,10},{10,8},{12,14},{14,12},{1,3},{3,1},... | collective-permute-start | bytes 1572872 | tf_op jit(solution)/shard_map/ppermute | solution.py:206
  190.4 20.8 %collective-permute-start.20 = (bf16[256,1024]{1,0:T(8,128)(2,1)S(1)}, bf16[256,1024]{1,0:T(8,128)(2,1)S(1)}, u32[]{:S(2)}, u32[]{:S(2)}) collective-permute-start(bf16[256,1024]{1,0:T(8,128)(2,1)S(1)} %add_convert_fusion.7), channel_id=1, source_target_pairs={{0,4},{2,6},{12,8},{14,10},{1,5},{3,7},{13,9},{15,11},{16,20},{18,... | collective-permute-start | bytes 1572872 | tf_op jit(solution)/shard_map/ppermute | solution.py:195
  194.0 19.0 %collective-permute-start.18 = (bf16[256,1024]{1,0:T(8,128)(2,1)S(1)}, bf16[256,1024]{1,0:T(8,128)(2,1)S(1)}, u32[]{:S(2)}, u32[]{:S(2)}) collective-permute-start(bf16[256,1024]{1,0:T(8,128)(2,1)S(1)} %add_convert_fusion.7), channel_id=1, source_target_pairs={{4,8},{6,10},{8,4},{10,6},{5,9},{7,11},{9,5},{11,7},{20,24},{22,26... | collective-permute-start | bytes 1572872 | tf_op jit(solution)/shard_map/ppermute | solution.py:195
  200.0 14.9 %collective-permute-start.15 = (bf16[256,1024]{1,0:T(8,128)(2,1)S(1)}, bf16[256,1024]{1,0:T(8,128)(2,1)S(1)}, u32[]{:S(2)}, u32[]{:S(2)}) collective-permute-start(bf16[256,1024]{1,0:T(8,128)(2,1)S(1)} %get-tuple-element.81), channel_id=1, source_target_pairs={{0,2},{2,0},{4,6},{6,4},{8,10},{10,8},{12,14},{14,12},{1,3},{3,1},... | collective-permute-start | bytes 1572872 | tf_op jit(solution)/shard_map/ppermute | solution.py:206
  201.7 17.1 %collective-permute-start.31 = (bf16[256,1024]{1,0:T(8,128)(2,1)S(1)}, bf16[256,1024]{1,0:T(8,128)(2,1)S(1)}, u32[]{:S(2)}, u32[]{:S(2)}) collective-permute-start(bf16[256,1024]{1,0:T(8,128)(2,1)S(1)} %add_convert_fusion), channel_id=1, source_target_pairs={{4,8},{6,10},{8,4},{10,6},{5,9},{7,11},{9,5},{11,7},{20,24},{22,26... | collective-permute-start | bytes 1572872 | tf_op jit(solution)/shard_map/ppermute | solution.py:195
  203.7 21.4 %collective-permute-start.29 = (bf16[256,1024]{1,0:T(8,128)(2,1)S(1)}, bf16[256,1024]{1,0:T(8,128)(2,1)S(1)}, u32[]{:S(2)}, u32[]{:S(2)}) collective-permute-start(bf16[256,1024]{1,0:T(8,128)(2,1)S(1)} %add_convert_fusion.1), channel_id=1, source_target_pairs={{0,4},{2,6},{4,0},{6,2},{8,12},{10,14},{12,8},{14,10},{1,5},{3,7},... | collective-permute-start | bytes 1572872 | tf_op jit(solution)/shard_map/ppermute | solution.py:195
  211.2 14.9 %collective-permute-start.26 = (bf16[256,1024]{1,0:T(8,128)(2,1)S(1)}, bf16[256,1024]{1,0:T(8,128)(2,1)S(1)}, u32[]{:S(2)}, u32[]{:S(2)}) collective-permute-start(bf16[256,1024]{1,0:T(8,128)(2,1)S(1)} %add_convert_fusion.4), channel_id=1, source_target_pairs={{0,2},{2,0},{4,6},{6,4},{8,10},{10,8},{12,14},{14,12},{1,3},{3,1},... | collective-permute-start | bytes 1572872 | tf_op jit(solution)/shard_map/ppermute | solution.py:206
  212.9 13.1 %collective-permute-start.21 = (bf16[256,1024]{1,0:T(8,128)(2,1)S(1)}, bf16[256,1024]{1,0:T(8,128)(2,1)S(1)}, u32[]{:S(2)}, u32[]{:S(2)}) collective-permute-start(bf16[256,1024]{1,0:T(8,128)(2,1)S(1)} %add_convert_fusion.5), channel_id=1, source_target_pairs={{4,8},{6,10},{8,4},{10,6},{5,9},{7,11},{9,5},{11,7},{20,24},{22,26... | collective-permute-start | bytes 1572872 | tf_op jit(solution)/shard_map/ppermute | solution.py:195
  215.1 15.7 %collective-permute-start.19 = (bf16[256,1024]{1,0:T(8,128)(2,1)S(1)}, bf16[256,1024]{1,0:T(8,128)(2,1)S(1)}, u32[]{:S(2)}, u32[]{:S(2)}) collective-permute-start(bf16[256,1024]{1,0:T(8,128)(2,1)S(1)} %add_convert_fusion.6), channel_id=1, source_target_pairs={{0,4},{2,6},{4,0},{6,2},{8,12},{10,14},{12,8},{14,10},{1,5},{3,7},... | collective-permute-start | bytes 1572872 | tf_op jit(solution)/shard_map/ppermute | solution.py:195
  218.8 15.2 %collective-permute-start.16 = (bf16[256,1024]{1,0:T(8,128)(2,1)S(1)}, bf16[256,1024]{1,0:T(8,128)(2,1)S(1)}, u32[]{:S(2)}, u32[]{:S(2)}) collective-permute-start(bf16[256,1024]{1,0:T(8,128)(2,1)S(1)} %get-tuple-element.82), channel_id=1, source_target_pairs={{0,2},{2,0},{4,6},{6,4},{8,10},{10,8},{12,14},{14,12},{1,3},{3,1},... | collective-permute-start | bytes 1572872 | tf_op jit(solution)/shard_map/ppermute | solution.py:206
  (10 other events, 142.4 us)
